TPU v7x, 32 devices: a whole 2x2x4 slice. The times are simulated.
32 devices in a mesh: det: 4 (over z), tm: 8 (over y, x, core).
Axes of the slice: x: 2, y: 2, z: 4, core: 2. Of those that a mesh axis runs over, the one named last changes fastest.
Arguments:
- iterate: float32 [16, 262144], P(None, ('det', 'tm')), may hold values from -6 to 6
- residual: float32 [16, 262144], P(None, ('det', 'tm')), may hold values from -40 to 40
- direction: float32 [16, 262144], P(None, ('det', 'tm')), may hold values from -2.5 to 2.5
- precond: float32 [262144], P(('det', 'tm')), may hold values from 0.02 to 0.12
- patch_ids: int32 [128, 64], P('det', 'tm'), may hold values from 0 to 4095, as said below
- pixel_in: int32 [128, 8192], P('det', 'tm'), may hold values from 0 to 63
- weights: float32 [128, 8192], P('det', 'tm'), may hold values from 0.5 to 1.5
- filter_diag: float32 [128], P('det'), may hold values from 1 to 1.5
- filter_band: float32 [128, 64], P('det'), may hold values from 0.003125 to 0.0075
Outputs:
- new_iterate: float32 [16, 262144], P(None, ('det', 'tm'))
- new_residual: float32 [16, 262144], P(None, ('det', 'tm'))
- new_direction: float32 [16, 262144], P(None, ('det', 'tm'))
Inputs may be any that keep to these rules, and one draw needn't show every extreme that they name: `patch_ids`: the blocks of one device (detectors 32 d0 .. and time blocks 8 t0 .. of its det index a and tm index c) name, for every owner o = a2 * 8 + c2, exactly 8 patches p with p // 128 = o.
All inputs are finite; a program needn't handle non-finite values.
Results may differ from a plain program's by a relative error of at most 0.0003.
Values sent between devices are 32-bit elements; how exact they have to be, the bound alone decides.
A program may use at most 64 MiB of HBM per device.

v0:
```python
import functools
import math

import jax
import jax.numpy as jnp
from jax import lax
from jax.experimental import pallas as pl
from jax.experimental.pallas import tpu as pltpu
from jax.sharding import PartitionSpec as P

PX = 64


def halves(values):
    top = values.astype(jnp.bfloat16)
    return top, (values - top.astype(jnp.float32)).astype(jnp.bfloat16)


def vmem(count):
    return [pl.BlockSpec(memory_space=pltpu.VMEM)] * count


def smem():
    return pl.BlockSpec(memory_space=pltpu.SMEM)


def peers_of(spans, devices):
    me = lax.axis_index("det") * spans + lax.axis_index("tm")
    stride = spans + 1 if math.gcd(spans + 1, devices) == 1 else 1

    def ahead(step):
        return lax.rem(me + step * stride, devices)

    def behind(step):
        return lax.rem(me + (devices - step) * stride, devices)

    def place(peer):
        return (peer // spans, lax.rem(peer, spans))

    return me, ahead, behind, place


def remote(src, dst, sent, got, device):
    return pltpu.make_async_remote_copy(
        src_ref=src,
        dst_ref=dst,
        send_sem=sent,
        recv_sem=got,
        device_id=device,
        device_id_type=pl.DeviceIdType.MESH,
    )


def greet(devices, ahead, place):
    barrier = pltpu.get_barrier_semaphore()

    @pl.loop(1, devices)
    def _(step):
        pl.semaphore_signal(
            barrier, inc=1, device_id=place(ahead(step)), device_id_type=pl.DeviceIdType.MESH
        )

    pl.semaphore_wait(barrier, devices - 1)


def fetch_kernel(
    spans, devices, slot_ref, ask_ref, table_ref, pixel_ref, gain_ref,
    asked_ref, line_ref, before_ref, after_ref,
    served, patches, numbers, head, tail,
    ask_sent, ask_got, sent, got, local, edge_sent, edge_got,
):
    me, ahead, behind, place = peers_of(spans, devices)
    per_owner = served.shape[1]
    rows, blocks, _ = pixel_ref.shape
    half = rows // 2
    greet(devices, ahead, place)

    def ask(step, slot):
        peer = ahead(step)
        return remote(
            ask_ref.at[peer], asked_ref.at[slot], ask_sent.at[step], ask_got.at[step], place(peer)
        )

    def give(step, slot):
        peer = ahead(step)
        return remote(
            served.at[peer],
            patches.at[pl.ds(slot * per_owner, per_owner)],
            sent.at[step],
            got.at[step],
            place(peer),
        )

    @pl.loop(1, devices)
    def _(step):
        ask(step, me).start()

    asked_ref[me] = ask_ref[me]

    @pl.loop(1, devices)
    def _(step):
        ask(step, behind(step)).wait_recv()

    move = pltpu.make_async_copy(asked_ref, numbers, local)
    move.start()
    move.wait()

    @pl.loop(1, devices)
    def _(step):
        peer = ahead(step)
        for i in range(per_owner):
            served[peer, i] = table_ref[numbers[peer, 0, i]]
        give(step, me).start()

    for i in range(per_owner):
        patches[me * per_owner + i] = table_ref[numbers[me, 0, i]]

    @pl.loop(1, devices)
    def _(step):
        ask(step, me).wait_send()
        give(step, me).wait_send()
        give(step, behind(step)).wait_recv()

    left = lax.broadcasted_iota(jnp.int32, (16, 128), 1) < 64

    def scan(d, wanted):
        pixels, gains = pixel_ref[d], gain_ref[d]
        made = []
        for j in wanted:
            pixel = jnp.broadcast_to(pixels[j : j + 1], (8, 128))
            gain = jnp.broadcast_to(gains[j : j + 1], (8, 128))
            patch = patches[slot_ref[d * blocks + j]]
            upper = jnp.take_along_axis(patch, pixel, axis=1) * gain
            lower = jnp.take_along_axis(patch, pixel + 64, axis=1) * gain
            line_ref[d, 16 * j : 16 * j + 8] = upper
            line_ref[d, 16 * j + 8 : 16 * j + 16] = lower
            made.append(jnp.concatenate([upper, lower], axis=0))
        return made

    @pl.loop(0, half)
    def _(d):
        first, last = scan(d, (0, blocks - 1))
        later_first, later_last = scan(d + half, (0, blocks - 1))
        head[d] = jnp.where(left, first, pltpu.roll(later_first, 64, 1))
        tail[d] = jnp.where(left, pltpu.roll(later_last, 64, 1), last)

    span = lax.axis_index("tm")
    group = lax.axis_index("det")
    forth = remote(
        tail, before_ref, edge_sent.at[0], edge_got.at[0],
        (group, lax.rem(span + 1, spans)),
    )
    back = remote(
        head, after_ref, edge_sent.at[1], edge_got.at[1],
        (group, lax.rem(span + spans - 1, spans)),
    )
    forth.start()
    back.start()

    @pl.loop(0, rows)
    def _(d):
        scan(d, range(1, blocks - 1))

    forth.wait()
    back.wait()

    @pl.when(span == 0)
    def _():
        before_ref[...] = jnp.zeros_like(before_ref)

    @pl.when(span == spans - 1)
    def _():
        after_ref[...] = jnp.zeros_like(after_ref)


def fetch(slot, ask, table, pixels, gains, per_owner, spans, devices):
    rows, blocks, _ = pixels.shape
    edge = (rows // 2, 16, 128)
    return pl.pallas_call(
        functools.partial(fetch_kernel, spans, devices),
        out_shape=(
            jax.ShapeDtypeStruct(ask.shape, jnp.int32),
            jax.ShapeDtypeStruct((rows, 16 * blocks, 128), jnp.float32),
            jax.ShapeDtypeStruct(edge, jnp.float32),
            jax.ShapeDtypeStruct(edge, jnp.float32),
        ),
        in_specs=[smem()] + vmem(4),
        out_specs=tuple(vmem(4)),
        scratch_shapes=[
            pltpu.VMEM((devices, per_owner, 8, 128), jnp.float32),
            pltpu.VMEM((devices * per_owner, 8, 128), jnp.float32),
            pltpu.SMEM(ask.shape, jnp.int32),
            pltpu.VMEM(edge, jnp.float32),
            pltpu.VMEM(edge, jnp.float32),
        ]
        + [pltpu.SemaphoreType.DMA((devices,))] * 4
        + [pltpu.SemaphoreType.DMA]
        + [pltpu.SemaphoreType.DMA((2,))] * 2,
        compiler_params=pltpu.CompilerParams(
            collective_id=1, has_side_effects=True, vmem_limit_bytes=32 * 1024 * 1024
        ),
    )(slot, ask, table, pixels, gains)


def swap_kernel(spans, devices, part_ref, out_ref, sent, got):
    me, ahead, behind, place = peers_of(spans, devices)
    greet(devices, ahead, place)

    def give(step, slot):
        peer = ahead(step)
        return remote(
            part_ref.at[peer], out_ref.at[slot], sent.at[step], got.at[step], place(peer)
        )

    @pl.loop(1, devices)
    def _(step):
        give(step, me).start()

    out_ref[me] = part_ref[me]

    @pl.loop(1, devices)
    def _(step):
        give(step, me).wait_send()
        give(step, behind(step)).wait_recv()


def swap(parts, spans, devices):
    return pl.pallas_call(
        functools.partial(swap_kernel, spans, devices),
        out_shape=jax.ShapeDtypeStruct(parts.shape, jnp.float32),
        in_specs=vmem(1),
        out_specs=vmem(1)[0],
        scratch_shapes=[pltpu.SemaphoreType.DMA((devices,))] * 2,
        compiler_params=pltpu.CompilerParams(
            collective_id=2, has_side_effects=True, vmem_limit_bytes=32 * 1024 * 1024
        ),
    )(parts)


def gather_up_kernel(asked_ref, parts_ref, out_ref, *others):
    chains = (out_ref,) + others
    share = parts_ref.shape[0] // len(chains)
    for chain in chains:
        chain[...] = jnp.zeros_like(chain)

    @pl.loop(0, share, unroll=4)
    def _(i):
        for c, chain in enumerate(chains):
            row = asked_ref[c * share + i]
            chain[row] = chain[row] + parts_ref[c * share + i]

    total = out_ref[...]
    for chain in others:
        total = total + chain[...]
    out_ref[...] = total


def gather_up(asked, parts, rows):
    return pl.pallas_call(
        gather_up_kernel,
        out_shape=jax.ShapeDtypeStruct((rows,) + parts.shape[1:], jnp.float32),
        in_specs=[smem()] + vmem(1),
        out_specs=vmem(1)[0],
        scratch_shapes=[pltpu.VMEM((rows,) + parts.shape[1:], jnp.float32)] * 3,
    )(asked, parts)


def project_kernel(
    slot_ref, line_ref, before_ref, after_ref, base_ref, pixel_ref, gain_ref, out_ref
):
    rows, blocks, _ = pixel_ref.shape
    half = rows // 2
    down = lax.broadcasted_iota(jnp.int32, (128, 128), 0)
    across = lax.broadcasted_iota(jnp.int32, (128, 128), 1)
    place = lax.broadcasted_iota(jnp.int32, (64, 128), 0)

    def one_row(d, before, after):
        base = jnp.broadcast_to(base_ref[d], (128, 256))
        turned = pltpu.roll(base, 0, 1, stride=1, stride_axis=0)
        near, far = turned[:, :128], turned[:, 128:]
        band = jnp.concatenate(
            [jnp.where(down > across, far, 0.0), near, jnp.where(down < across, far, 0.0)], axis=0
        )
        band_top, band_low = halves(band)
        cells = jnp.concatenate([before, line_ref[d], after], axis=0)
        top, low = halves(cells)
        wide_top = jnp.concatenate(
            [top[16 * o : 16 * (o + blocks)] for o in range(3)], axis=1
        )
        wide_low = jnp.concatenate(
            [low[16 * o : 16 * (o + blocks)] for o in range(3)], axis=1
        )
        filtered = (
            jnp.dot(wide_top, band_top, preferred_element_type=jnp.float32)
            + jnp.dot(wide_low, band_top, preferred_element_type=jnp.float32)
            + jnp.dot(wide_top, band_low, preferred_element_type=jnp.float32)
        )
        pixels, gains = pixel_ref[d], gain_ref[d]
        for j in range(blocks):
            gain = jnp.broadcast_to(gains[j : j + 1], (16, 128))
            pixel = jnp.broadcast_to(pixels[j : j + 1], (64, 128))
            hot = jnp.where(place == pixel, 1.0, 0.0).astype(jnp.bfloat16)
            both = jnp.concatenate(halves(filtered[16 * j : 16 * j + 16] * gain), axis=0)
            added = lax.dot_general(
                both, hot, (((1,), (1,)), ((), ())), preferred_element_type=jnp.float32
            )
            added = added[:16] + added[16:]
            out_ref[slot_ref[d * blocks + j]] = jnp.concatenate([added[:8], added[8:]], axis=1)

    @pl.loop(0, half, unroll=2)
    def _(d):
        before, after = before_ref[d], after_ref[d]
        one_row(d, before, after)
        one_row(d + half, pltpu.roll(before, 64, 1), pltpu.roll(after, 64, 1))


def project(slot, line, before, after, base, pixel, gain):
    rows, blocks, _ = pixel.shape
    return pl.pallas_call(
        project_kernel,
        out_shape=jax.ShapeDtypeStruct((rows * blocks, 8, 128), jnp.float32),
        in_specs=[smem()] + vmem(6),
        out_specs=vmem(1)[0],
        compiler_params=pltpu.CompilerParams(vmem_limit_bytes=40 * 1024 * 1024),
    )(slot, line, before, after, base, pixel, gain)


def factors_kernel(
    spans, devices, old_ref, way_ref, scale_ref, image_ref, out_ref, part, held, sent, got
):
    me, ahead, behind, place = peers_of(spans, devices)
    barrier = pltpu.get_barrier_semaphore()

    @pl.loop(1, devices)
    def _(step):
        pl.semaphore_signal(
            barrier, inc=1, device_id=place(ahead(step)), device_id_type=pl.DeviceIdType.MESH
        )

    image = image_ref[...]
    lean = scale_ref[...] * old_ref[...]
    columns = (
        jnp.sum(old_ref[...] * lean, axis=1, keepdims=True),
        jnp.sum(way_ref[...] * image, axis=1, keepdims=True),
        jnp.sum(image * lean, axis=1, keepdims=True),
        jnp.sum(image * (scale_ref[...] * image), axis=1, keepdims=True),
    )
    lane = lax.broadcasted_iota(jnp.int32, part.shape, 1)
    tile = jnp.zeros(part.shape, jnp.float32)
    for i, column in enumerate(columns):
        tile = jnp.where(lane == i, column, tile)
    part[...] = tile
    held[me] = tile
    pl.semaphore_wait(barrier, devices - 1)

    def give(step, slot):
        return remote(
            part, held.at[slot], sent.at[step], got.at[step], place(ahead(step))
        )

    @pl.loop(1, devices)
    def _(step):
        give(step, me).start()

    @pl.loop(1, devices)
    def _(step):
        give(step, me).wait_send()
        give(step, behind(step)).wait_recv()

    total = jnp.sum(held[...], axis=0)
    norm_old, curvature, cross, square = (total[:, i : i + 1] for i in range(4))
    step_size = norm_old / curvature
    norm_new = norm_old - step_size * (2.0 * cross - step_size * square)
    out_ref[...] = jnp.where(lane == 0, step_size, norm_new / norm_old)


def factors(residual, direction, precond, image, spans, devices):
    tile = (residual.shape[0], 128)
    return pl.pallas_call(
        functools.partial(factors_kernel, spans, devices),
        out_shape=jax.ShapeDtypeStruct(tile, jnp.float32),
        in_specs=vmem(4),
        out_specs=vmem(1)[0],
        scratch_shapes=[
            pltpu.VMEM(tile, jnp.float32),
            pltpu.VMEM((devices,) + tile, jnp.float32),
            pltpu.SemaphoreType.DMA((devices,)),
            pltpu.SemaphoreType.DMA((devices,)),
        ],
        compiler_params=pltpu.CompilerParams(
            collective_id=0, has_side_effects=True, vmem_limit_bytes=32 * 1024 * 1024
        ),
    )(residual, direction, precond, image)


def per_device(
    iterate, residual, direction, precond, patch_ids, pixel_in, weights, filter_diag, filter_band
):
    probes = iterate.shape[0]
    det_rows, time_blocks = patch_ids.shape
    half_band = filter_band.shape[1]
    groups = lax.axis_size("det")
    spans = lax.axis_size("tm")
    devices = groups * spans
    blocks = det_rows * time_blocks
    per_owner = blocks // devices
    own_patches = iterate.shape[1] // PX
    patch_flat = patch_ids.reshape(blocks)
    owners = patch_flat // own_patches
    numbers = jnp.arange(blocks, dtype=jnp.int32)
    earlier = (owners[:, None] == owners[None, :]) & (numbers[None, :] < numbers[:, None])
    slot = owners * per_owner + jnp.sum(earlier.astype(jnp.int32), axis=1)
    requests = jnp.sum(
        jnp.where(numbers[:, None] == slot[None, :], (patch_flat % own_patches)[None, :], 0), axis=1
    ).reshape(devices, per_owner)
    requests = jnp.pad(requests, ((0, 0), (0, 128 - per_owner)))[:, None, :]
    table = (
        direction.reshape(2, 8, own_patches, PX).transpose(2, 1, 0, 3).reshape(own_patches, 8, 128)
    )
    pixels = pixel_in.reshape(det_rows, time_blocks, 128)
    gains = weights.reshape(det_rows, time_blocks, 128)
    asked, line, before, after = fetch(
        slot, requests, table, pixels, gains, per_owner, spans, devices
    )
    asked = asked[:, 0, :per_owner].reshape(blocks)
    base = jnp.concatenate(
        [
            filter_diag[:, None],
            filter_band,
            jnp.zeros((det_rows, 255 - 2 * half_band), jnp.float32),
            filter_band[:, ::-1],
        ],
        axis=1,
    )[:, None, :]
    parts = project(slot, line, before, after, base, pixels, gains)
    collected = swap(parts.reshape(devices, per_owner, 8, 128), spans, devices)
    collected = collected.reshape(blocks, 8, 128)
    image_map = (
        gather_up(asked, collected, own_patches)
        .reshape(own_patches, 8, 2, PX)
        .transpose(2, 1, 0, 3)
        .reshape(probes, own_patches * PX)
    )
    factor = factors(residual, direction, precond[None, :], image_map, spans, devices)
    step_size, ratio = factor[:, 0:1], factor[:, 1:2]
    new_iterate = iterate + step_size * direction
    new_residual = residual - step_size * image_map
    new_direction = precond * new_residual + ratio * direction
    return (new_iterate, new_residual, new_direction)


def solution(mesh):
    in_specs = (
        P(None, ("det", "tm")),
        P(None, ("det", "tm")),
        P(None, ("det", "tm")),
        P(("det", "tm")),
        P("det", "tm"),
        P("det", "tm"),
        P("det", "tm"),
        P("det"),
        P("det", None),
    )
    out_specs = (P(None, ("det", "tm")), P(None, ("det", "tm")), P(None, ("det", "tm")))
    return jax.shard_map(
        per_device, mesh=mesh, in_specs=in_specs, out_specs=out_specs, check_vma=False
    )
```

profile of v0, /device:TPU:0, one launch (start us, length us, event | category | flops | bytes accessed | tf_op | source)
XLA Modules:
  0.0 113.5 jit_solution(4959460961327200575)
XLA Ops:
  0.6 0.1 pad.7.clone
  0.7 0.8 copy.21
  1.5 0.1 reshape.127
  1.6 0.2 convert_reduce_fusion
  1.8 0.1 select_reduce_fusion
  1.9 0.1 reshape.128
  2.0 0.7 copy.24
  2.7 0.8 rev.3
  3.5 0.8 pad_maximum_fusion
  4.4 0.9 copy.27
  5.3 0.9 copy.28
  6.2 1.5 %reshape.129 = f32[2,8,128,64]{3,2,1,0:T(8,128)S(1)} reshape(f32[16,8192]{1,0:T(8,128)} %way_ref.1) | data formatting | bytes 1048576 | tf_op jit(solution)/shard_map/reshape | solution.py:418
  7.7 0.3 copy.22
  8.0 0.2 copy.23.table_ref
  8.3 44.5 %shard_map.112 = (s32[32,1,128]{2,1,0:T(1,128)S(1)}, f32[32,128,128]{2,1,0:T(8,128)S(1)}, f32[16,16,128]{2,1,0:T(8,128)S(1)}, f32[16,16,128]{2,1,0:T(8,128)S(1)}) custom-call(s32[256]{0:T(256)S(1)} %multiply_add_fusion.2.slot_ref, s32[32,1,128]{2,1,0:T(1,128)S(1)} %bitcast.23, f32[128,8,128]{2,1,0:T(8,128)S(1)} %copy.23.table_ref, ...), custom_call_target="tpu_custom_call" | custom-call | tf_op jit(solution)/shard_map/pallas_call | solution.py:179
  52.8 0.7 reshape_squeeze.3.asked_ref
  53.5 11.8 %shard_map.113 = f32[256,8,128]{2,1,0:T(8,128)S(1)} custom-call(s32[256]{0:T(256)S(1)} %multiply_add_fusion.2.slot_ref, f32[32,128,128]{2,1,0:T(8,128)S(1)} %get-tuple-element.8.line_ref, f32[16,16,128]{2,1,0:T(8,128)S(1)} %get-tuple-element.9.before_ref, f32[16,16,128]{2,1,0:T(8,128)S(1)} %get-tuple-element.10.after_ref, ...), custom_call_target="tpu_custom_call" | custom-call | tf_op jit(solution)/shard_map/pallas_call | solution.py:319
  65.3 28.2 %shard_map.114 = f32[32,8,8,128]{3,2,1,0:T(8,128)S(1)} custom-call(f32[32,8,8,128]{3,2,1,0:T(8,128)S(1)} %bitcast.17), custom_call_target="tpu_custom_call" | custom-call | tf_op jit(solution)/shard_map/pallas_call | solution.py:228
  93.5 0.0 copy-start.1
  93.5 1.0 copy-done.1
  94.5 2.7 %shard_map.115 = f32[128,8,128]{2,1,0:T(8,128)} custom-call(s32[256]{0:T(256)} %reshape_squeeze.3.asked_ref, f32[256,8,128]{2,1,0:T(8,128)} %bitcast.16), custom_call_target="tpu_custom_call" | custom-call | tf_op jit(solution)/shard_map/pallas_call | solution.py:259
  97.2 0.0 copy-start
  97.2 0.0 copy-start.2
  97.2 0.0 copy-start.3
  97.2 1.3 %copy.25 = f32[128,8,128]{0,2,1:T(8,128)S(1)} copy(f32[128,8,128]{2,1,0:T(8,128)} %shard_map.115) | data formatting | bytes 1048576 | tf_op jit(solution)/shard_map/pallas_call | solution.py:259
  98.5 0.0 copy-start.4
  98.5 0.3 copy.26
  98.9 0.4 reshape.136.image_ref
  99.2 0.0 copy-done
  99.2 0.0 copy-done.2
  99.2 0.0 copy-done.3
  99.2 12.7 %shard_map.116 = f32[16,128]{1,0:T(8,128)S(1)} custom-call(f32[16,8192]{1,0:T(8,128)S(1)} %copy-done.2, f32[16,8192]{1,0:T(8,128)S(1)} %copy-done, f32[1,8192]{1,0:T(1,128)S(1)} %bitcast.22, f32[16,8192]{1,0:T(8,128)S(1)} %reshape.136.image_ref), custom_call_target="tpu_custom_call" | custom-call | tf_op jit(solution)/shard_map/pallas_call | solution.py:379
  112.0 0.2 slice_reduce_fusion.1
  112.1 0.0 copy-done.4
  112.2 1.3 %multiply_add_fusion = (f32[16,8192]{1,0:T(8,128)}, f32[16,8192]{1,0:T(8,128)}, f32[16,8192]{1,0:T(8,128)}) fusion(f32[16,8192]{1,0:T(8,128)S(1)} %copy-done, f32[16]{0:T(128)S(1)} %get-tuple-element.11, f32[8192]{0:T(1024)S(1)} %copy-done.3, f32[16,8192]{1,0:T(8,128)S(1)} %copy-done.2, f32[16,8192]{1,0:T(8,128)S(1)} %reshape.136.image_ref, ...), kind=kLoop, calls=%fused_computation | loop fusion | flops 917504 | bytes 3702912 | tf_op jit(solution)/shard_map/add | solution.py:448
  (6 shorter events, 0.1 us)
Async XLA Ops:
  93.5 1.0 copy-start.1
  97.2 2.1 %copy-start = (f32[16,8192]{1,0:T(8,128)S(1)}, f32[16,8192]{1,0:T(8,128)}, u32[]{:S(2)}) copy-start(f32[16,8192]{1,0:T(8,128)} %way_ref.1) | copy-start | bytes 1572868
  97.2 2.1 %copy-start.2 = (f32[16,8192]{1,0:T(8,128)S(1)}, f32[16,8192]{1,0:T(8,128)}, u32[]{:S(2)}) copy-start(f32[16,8192]{1,0:T(8,128)} %old_ref.1) | copy-start | bytes 1572868
  97.2 2.1 %copy-start.3 = (f32[8192]{0:T(1024)S(1)}, f32[8192]{0:T(1024)}, u32[]{:S(2)}) copy-start(f32[8192]{0:T(1024)} %param.12) | copy-start | bytes 98308
  98.5 13.6 %copy-start.4 = (f32[16,8192]{1,0:T(8,128)S(1)}, f32[16,8192]{1,0:T(8,128)}, u32[]{:S(2)}) copy-start(f32[16,8192]{1,0:T(8,128)} %param.9) | copy-start | bytes 1572868
where the time goes:
time: 114 us; the launch traced here: 113 us
  Pallas kernels  99.9 us (88%)
  local copies, waits for them, and re-layouts  10.3 us (9%)
  other arithmetic  2.42 us (2%)
    pallas_call x1, Pallas kernels, fetch(): pl.pallas_call(functools.partial(fetch_kernel, spans, devices), out_shape...  44.5 us
    pallas_call x1, Pallas kernels, swap(): pl.pallas_call(functools.partial(swap_kernel, spans, devices), out_shape=...  28.2 us
    pallas_call x1, Pallas kernels, factors(): pl.pallas_call(functools.partial(factors_kernel, spans, devices), out_sha...  12.7 us
    pallas_call x1, Pallas kernels, project(): pl.pallas_call(project_kernel, out_shape=jax.ShapeDtypeStruct((rows * blo...  11.8 us
    unnamed x13, local copies, waits for them, and re-layouts  3.62 us
    pallas_call x1, Pallas kernels, gather_up(): pl.pallas_call(gather_up_kernel, out_shape=jax.ShapeDtypeStruct((rows,) +...  2.65 us

commit v1 on v0

v1 whole, which is shorter than its diff:
```python
import functools
import math

import jax
import jax.numpy as jnp
from jax import lax
from jax.experimental import pallas as pl
from jax.experimental.pallas import tpu as pltpu
from jax.sharding import PartitionSpec as P

PX = 64
MESH = pl.DeviceIdType.MESH


def halves(values):
    top = values.astype(jnp.bfloat16)
    return top, (values - top.astype(jnp.float32)).astype(jnp.bfloat16)


def vmem(count):
    return [pl.BlockSpec(memory_space=pltpu.VMEM)] * count


def smem(count):
    return [pl.BlockSpec(memory_space=pltpu.SMEM)] * count


def peers_of(spans, devices):
    me = lax.axis_index("det") * spans + lax.axis_index("tm")
    stride = spans + 1 if math.gcd(spans + 1, devices) == 1 else 1

    def ahead(step):
        return lax.rem(me + step * stride, devices)

    def behind(step):
        return lax.rem(me + (devices - step) * stride, devices)

    def place(peer):
        return (peer // spans, lax.rem(peer, spans))

    return me, ahead, behind, place


def remote(src, dst, sent, got, device):
    return pltpu.make_async_remote_copy(
        src_ref=src, dst_ref=dst, send_sem=sent, recv_sem=got, device_id=device, device_id_type=MESH
    )


def step_kernel(
    spans, devices,
    slot_ref, block_ref, diag_ref, ask_ref, way_ref, old_ref, scale_ref, pixel_ref, gain_ref, band_ref,
    image_ref, factor_ref,
    asked, numbers, table, served, patches, pixels, turned, gains, turned_gains, line, bands, hot,
    head, tail, before, after, cells, part, collected, spread, image, sums, held,
    ask_sent, ask_got, sent, got, local, edge_sent, edge_got, back_sent, back_got, sum_sent, sum_got,
):
    me, ahead, behind, place = peers_of(spans, devices)
    span, group = lax.axis_index("tm"), lax.axis_index("det")
    rows = pixel_ref.shape[0]
    blocks = block_ref.shape[0]
    per_row = blocks // rows
    per_owner = blocks // devices
    pairs = per_owner // 2
    half = rows // 2
    tiles = way_ref.shape[1] // 128
    deep = pairs * 8
    left = lax.broadcasted_iota(jnp.int32, (8, 128), 1) < 64

    barrier = pltpu.get_barrier_semaphore()

    @pl.loop(1, devices)
    def _(step):
        pl.semaphore_signal(barrier, inc=1, device_id=place(ahead(step)), device_id_type=MESH)

    @pl.loop(0, tiles, unroll=2)
    def _(q):
        for h in range(2):
            tile = way_ref[8 * h : 8 * h + 8, pl.ds(pl.multiple_of(q * 128, 128), 128)]
            table[0, h, q] = tile
            table[1, h, q] = pltpu.roll(tile, 64, 1)

    pl.semaphore_wait(barrier, devices - 1)

    def ask(step, slot):
        peer = ahead(step)
        return remote(
            ask_ref.at[peer], asked.at[slot], ask_sent.at[step], ask_got.at[step], place(peer)
        )

    def give(h, step, slot):
        peer = ahead(step)
        return remote(
            served.at[h, peer], patches.at[h, slot], sent.at[h, step], got.at[h, step], place(peer)
        )

    @pl.loop(1, devices)
    def _(step):
        ask(step, me).start()

    asked[me] = ask_ref[me]

    for r in range(0, rows, 8):
        for j in range(per_row):
            these = pl.ds(r * per_row + j, 8, stride=per_row)
            pixel = pixel_ref[r : r + 8, 128 * j : 128 * j + 128]
            gain = gain_ref[r : r + 8, 128 * j : 128 * j + 128]
            pixels[these, :] = pixel
            turned[these, :] = pltpu.roll(pixel, 64, 1)
            gains[these, :] = gain
            turned_gains[these, :] = pltpu.roll(gain, 64, 1)

    @pl.loop(1, devices)
    def _(step):
        ask(step, behind(step)).wait_recv()

    move = pltpu.make_async_copy(asked, numbers, local)
    move.start()
    move.wait()

    def serve(h, peer, dst):
        for i in range(pairs):
            a, b = numbers[peer, 0, 2 * i], numbers[peer, 0, 2 * i + 1]
            dst[h, peer, i] = jnp.where(left, table[a & 1, h, a >> 1], table[1 - (b & 1), h, b >> 1])

    for h in range(2):

        @pl.loop(1, devices)
        def _(step):
            serve(h, ahead(step), served)
            give(h, step, me).start()

        serve(h, me, patches)

    lane = lax.broadcasted_iota(jnp.int32, (1, 128), 1)
    band = jnp.concatenate([band_ref[...], jnp.zeros((rows, 128 - band_ref.shape[1]), jnp.float32)], axis=1)
    wanted = jnp.broadcast_to(jnp.where(lane < 64, 63 - lane, jnp.maximum(lane - 65, 0)), (rows, 128))
    upper = jnp.take_along_axis(band, wanted, axis=1)
    lower = jnp.where(
        lane == 0, jnp.take_along_axis(band, jnp.full((rows, 128), 63, jnp.int32), axis=1), 0.0
    )
    sums[...] = jnp.zeros_like(sums)
    cells_of_band = jnp.concatenate([lower, upper], axis=1)
    held_bands = cells_of_band

    wide_lane = lax.broadcasted_iota(jnp.int32, (1, 256), 1)
    for d in range(rows):
        base = jnp.where(wide_lane == 192, diag_ref[d], held_bands[d : d + 1])
        around = pltpu.roll(jnp.broadcast_to(base, (128, 256)), 0, 1, stride=1, stride_axis=0)
        bands[d] = jnp.concatenate(
            [
                jnp.concatenate(halves(around[:, :128]), axis=1),
                jnp.concatenate(halves(around[:, 128:]), axis=1),
            ],
            axis=0,
        )

    spot = lax.broadcasted_iota(jnp.int32, (PX, 128), 0)

    @pl.loop(0, blocks, unroll=2)
    def _(s):
        pixel = jnp.broadcast_to(pixels[pl.ds(block_ref[s], 1), :], (PX, 128))
        hot[s] = jnp.where(spot == pixel, 1.0, 0.0).astype(jnp.bfloat16)

    asks = asked[:, 0, :]
    even = jnp.concatenate(
        [jnp.broadcast_to(asks[:, 2 * i : 2 * i + 1], (devices, 2 * tiles)) for i in range(pairs)], axis=0
    )
    odd = jnp.concatenate(
        [jnp.broadcast_to(asks[:, 2 * i + 1 : 2 * i + 2], (devices, 2 * tiles)) for i in range(pairs)], axis=0
    )
    column = lax.broadcasted_iota(jnp.int32, even.shape, 1)
    first = column < tiles
    target = jnp.where(first, 2 * column, 2 * (column - tiles) + 1)
    straight = jnp.where(jnp.where(first, even, odd) == target, 1.0, 0.0)
    crossed = jnp.where(jnp.where(first, odd, even) == target, 1.0, 0.0)
    spread[...] = jnp.concatenate([straight.T, crossed.T], axis=1).astype(jnp.bfloat16)

    def scan(h, peer):
        for i in range(pairs):
            patch = patches[h, peer, i]
            for side in range(2):
                s = peer * per_owner + 2 * i + side
                b = block_ref[s]
                pixel = jnp.broadcast_to(turned[pl.ds(b, 1), :], (8, 128)) + 64 * side
                gain = jnp.broadcast_to(turned_gains[pl.ds(b, 1), :], (8, 128))
                line[h, s] = jnp.take_along_axis(patch, pixel, axis=1) * gain

    def arrive(h, low, high):
        @pl.loop(low, high)
        def _(step):
            give(h, step, behind(step)).wait_recv()
            scan(h, behind(step))

    forth = [
        remote(tail.at[h], before.at[h], edge_sent.at[h, 0], edge_got.at[h, 0],
               (group, lax.rem(span + 1, spans)))
        for h in range(2)
    ]
    back = [
        remote(head.at[h], after.at[h], edge_sent.at[h, 1], edge_got.at[h, 1],
               (group, lax.rem(span + spans - 1, spans)))
        for h in range(2)
    ]

    def edges(h):
        @pl.loop(0, half)
        def _(d):
            start, end = d * per_row, d * per_row + per_row - 1
            far = half * per_row
            head[h, d] = jnp.where(
                left, pltpu.roll(line[h, slot_ref[start]], 64, 1), line[h, slot_ref[start + far]]
            )
            tail[h, d] = jnp.where(
                left, line[h, slot_ref[end]], pltpu.roll(line[h, slot_ref[end + far]], 64, 1)
            )

        forth[h].start()
        back[h].start()

    def edges_in(h):
        forth[h].wait()
        back[h].wait()

        @pl.when(span == 0)
        def _():
            before[h] = jnp.zeros_like(before[h])

        @pl.when(span == spans - 1)
        def _():
            after[h] = jnp.zeros_like(after[h])

    def one_row(h, d, early, late):
        mine = [early] + [line[h, slot_ref[d * per_row + j]] for j in range(per_row)] + [late]
        shifted = [jnp.where(left, mine[m], mine[m + 1]) for m in range(per_row + 1)]
        near = jnp.concatenate(shifted[:-1], axis=0)
        far = jnp.concatenate(shifted[1:], axis=0)
        wide = jnp.concatenate(
            [jnp.concatenate(halves(near), axis=0), jnp.concatenate(halves(far), axis=0)], axis=1
        )
        made = jnp.dot(wide, bands[d], preferred_element_type=jnp.float32)
        n = 8 * per_row
        filtered = made[:n, :128] + (made[n:, :128] + made[:n, 128:])
        for j in range(per_row):
            gain = jnp.broadcast_to(gains[pl.ds(d * per_row + j, 1), :], (8, 128))
            values = filtered[8 * j : 8 * j + 8] * gain
            top = values.astype(jnp.bfloat16).astype(jnp.float32)
            cells[h, d * per_row + j] = jnp.concatenate([top, values - top], axis=0).astype(jnp.bfloat16)

    def filter_all(h):
        @pl.loop(0, half)
        def _(d):
            early, late = before[h, d], after[h, d]
            one_row(h, d, early, pltpu.roll(late, 64, 1))
            one_row(h, d + half, pltpu.roll(early, 64, 1), late)

    blank = jnp.zeros((PX, 128), jnp.bfloat16)

    def project(h, peer, dst, where):
        for i in range(pairs):
            s = peer * per_owner + 2 * i
            both = jnp.concatenate([cells[h, block_ref[s]], cells[h, block_ref[s + 1]]], axis=1)
            grid = jnp.concatenate(
                [
                    jnp.concatenate([hot[s], blank], axis=1),
                    jnp.concatenate([blank, hot[s + 1]], axis=1),
                ],
                axis=0,
            )
            added = lax.dot_general(
                both, grid, (((1,), (1,)), ((), ())), preferred_element_type=jnp.float32
            )
            dst[pl.ds(pl.multiple_of(where + 8 * i, 8), 8), :] = added[:8] + added[8:]

    def rows_of(h, slot):
        return pl.ds(pl.multiple_of((h * devices + slot) * deep, 8), deep)

    def send_back(h, step, slot):
        peer = ahead(step)
        return remote(
            part.at[rows_of(h, peer)], collected.at[rows_of(h, slot)],
            back_sent.at[h, step], back_got.at[h, step], place(peer),
        )

    def project_all(h):
        @pl.loop(1, devices)
        def _(step):
            peer = ahead(step)
            project(h, peer, part, (h * devices + peer) * deep)
            send_back(h, step, me).start()

        project(h, me, collected, (h * devices + me) * deep)

    def gather_up(h):
        @pl.loop(1, devices)
        def _(step):
            send_back(h, step, behind(step)).wait_recv()

        wide_left = lax.broadcasted_iota(jnp.int32, (tiles, 128), 1) < 64
        for k in range(8):
            came = jnp.concatenate(
                [
                    collected[pl.ds(h * devices * deep + 8 * i + k, devices, stride=deep), :]
                    for i in range(pairs)
                ],
                axis=0,
            )
            came = jnp.concatenate([came, pltpu.roll(came, 64, 1)], axis=0)
            total = jnp.dot(
                spread[...], jnp.concatenate(halves(came), axis=1), preferred_element_type=jnp.float32
            )
            total = total[:, :128] + total[:, 128:]
            image[pl.ds(h * tiles * 8 + k, tiles, stride=8), :] = jnp.where(
                wide_left, total[:tiles], total[tiles:]
            )

        zero = jnp.zeros((8, 128), jnp.float32)

        def add(q, totals):
            these = pl.ds(pl.multiple_of(q * 128, 128), 128)
            tile = image[pl.ds(pl.multiple_of((h * tiles + q) * 8, 8), 8), :]
            image_ref[8 * h : 8 * h + 8, these] = tile
            old = old_ref[8 * h : 8 * h + 8, these]
            scale = jnp.broadcast_to(scale_ref[:, these], (8, 128))
            way = way_ref[8 * h : 8 * h + 8, these]
            lean = scale * old
            return (
                totals[0] + old * lean,
                totals[1] + way * tile,
                totals[2] + tile * lean,
                totals[3] + tile * (scale * tile),
            )

        totals = lax.fori_loop(0, tiles, add, (zero,) * 4, unroll=4)
        whole = sums[...]
        lanes = lax.broadcasted_iota(jnp.int32, (8, 128), 1)
        for i, total in enumerate(totals):
            whole = jnp.where(lanes == 4 * h + i, jnp.sum(total, axis=1, keepdims=True), whole)
        sums[...] = whole

    scan(0, me)
    arrive(0, 1, devices)
    edges(0)
    scan(1, me)
    arrive(1, 1, devices // 2)
    edges_in(0)
    filter_all(0)
    arrive(1, devices // 2, devices)
    edges(1)
    project_all(0)
    edges_in(1)
    filter_all(1)
    project_all(1)

    @pl.loop(1, devices)
    def _(step):
        ask(step, me).wait_send()
        give(0, step, me).wait_send()
        give(1, step, me).wait_send()

    gather_up(0)
    gather_up(1)

    def give_sums(step, slot):
        return remote(sums, held.at[slot], sum_sent.at[step], sum_got.at[step], place(ahead(step)))

    @pl.loop(1, devices)
    def _(step):
        give_sums(step, me).start()

    held[me] = sums[...]

    @pl.loop(1, devices)
    def _(step):
        send_back(0, step, me).wait_send()
        send_back(1, step, me).wait_send()
        give_sums(step, me).wait_send()
        give_sums(step, behind(step)).wait_recv()

    total = jnp.sum(held[...], axis=0)
    for h in range(2):
        norm_old, curvature, cross, square = (total[:, 4 * h + i : 4 * h + i + 1] for i in range(4))
        step_size = norm_old / curvature
        norm_new = norm_old - step_size * (2.0 * cross - step_size * square)
        lanes = lax.broadcasted_iota(jnp.int32, (8, 128), 1)
        factor_ref[8 * h : 8 * h + 8, :] = jnp.where(lanes == 0, step_size, norm_new / norm_old)


def one_step(slot, block, diag, ask, way, old, scale, pixels, gains, band, spans, devices):
    blocks = slot.shape[0]
    rows = pixels.shape[0]
    per_owner = blocks // devices
    pairs = per_owner // 2
    tiles = way.shape[1] // 128
    edge = (2, rows // 2, 8, 128)
    both = (2, devices, pairs, 8, 128)
    flat = (2 * devices * pairs * 8, 128)
    dma = pltpu.SemaphoreType.DMA
    return pl.pallas_call(
        functools.partial(step_kernel, spans, devices),
        out_shape=(
            jax.ShapeDtypeStruct(way.shape, jnp.float32),
            jax.ShapeDtypeStruct((way.shape[0], 128), jnp.float32),
        ),
        in_specs=smem(3) + vmem(7),
        out_specs=tuple(vmem(2)),
        scratch_shapes=[
            pltpu.VMEM(ask.shape, jnp.int32),
            pltpu.SMEM(ask.shape, jnp.int32),
            pltpu.VMEM((2, 2, tiles, 8, 128), jnp.float32),
            pltpu.VMEM(both, jnp.float32),
            pltpu.VMEM(both, jnp.float32),
            pltpu.VMEM((blocks, 128), jnp.int32),
            pltpu.VMEM((blocks, 128), jnp.int32),
            pltpu.VMEM((blocks, 128), jnp.float32),
            pltpu.VMEM((blocks, 128), jnp.float32),
            pltpu.VMEM((2, blocks, 8, 128), jnp.float32),
            pltpu.VMEM((rows, 256, 256), jnp.bfloat16),
            pltpu.VMEM((blocks, PX, 128), jnp.bfloat16),
            pltpu.VMEM(edge, jnp.float32),
            pltpu.VMEM(edge, jnp.float32),
            pltpu.VMEM(edge, jnp.float32),
            pltpu.VMEM(edge, jnp.float32),
            pltpu.VMEM((2, blocks, 16, 128), jnp.bfloat16),
            pltpu.VMEM(flat, jnp.float32),
            pltpu.VMEM(flat, jnp.float32),
            pltpu.VMEM((2 * tiles, blocks), jnp.bfloat16),
            pltpu.VMEM((2 * tiles * 8, 128), jnp.float32),
            pltpu.VMEM((8, 128), jnp.float32),
            pltpu.VMEM((devices, 8, 128), jnp.float32),
            dma((devices,)),
            dma((devices,)),
            dma((2, devices)),
            dma((2, devices)),
            dma,
            dma((2, 2)),
            dma((2, 2)),
            dma((2, devices)),
            dma((2, devices)),
            dma((devices,)),
            dma((devices,)),
        ],
        compiler_params=pltpu.CompilerParams(
            collective_id=0, has_side_effects=True, vmem_limit_bytes=48 * 1024 * 1024
        ),
    )(slot, block, diag, ask, way, old, scale, pixels, gains, band)


def per_device(
    iterate, residual, direction, precond, patch_ids, pixel_in, weights, filter_diag, filter_band
):
    det_rows, time_blocks = patch_ids.shape
    spans = lax.axis_size("tm")
    devices = lax.axis_size("det") * spans
    blocks = det_rows * time_blocks
    per_owner = blocks // devices
    own_patches = iterate.shape[1] // PX
    patch_flat = patch_ids.reshape(blocks)
    owners = patch_flat // own_patches
    numbers = jnp.arange(blocks, dtype=jnp.int32)
    earlier = (owners[:, None] == owners[None, :]) & (numbers[None, :] < numbers[:, None])
    slot = owners * per_owner + jnp.sum(earlier.astype(jnp.int32), axis=1)
    packed = numbers * own_patches + patch_flat % own_patches
    by_slot = jnp.sum(jnp.where(numbers[:, None] == slot[None, :], packed[None, :], 0), axis=1)
    block = by_slot // own_patches
    requests = (by_slot % own_patches).reshape(devices, per_owner)
    requests = jnp.pad(requests, ((0, 0), (0, 128 - per_owner)))[:, None, :]
    image_map, factor = one_step(
        slot, block, filter_diag, requests, direction, residual, precond[None, :],
        pixel_in, weights, filter_band, spans, devices,
    )
    step_size, ratio = factor[:, 0:1], factor[:, 1:2]
    new_iterate = iterate + step_size * direction
    new_residual = residual - step_size * image_map
    new_direction = precond * new_residual + ratio * direction
    return (new_iterate, new_residual, new_direction)


def solution(mesh):
    in_specs = (
        P(None, ("det", "tm")),
        P(None, ("det", "tm")),
        P(None, ("det", "tm")),
        P(("det", "tm")),
        P("det", "tm"),
        P("det", "tm"),
        P("det", "tm"),
        P("det"),
        P("det", None),
    )
    out_specs = (P(None, ("det", "tm")), P(None, ("det", "tm")), P(None, ("det", "tm")))
    return jax.shard_map(
        per_device, mesh=mesh, in_specs=in_specs, out_specs=out_specs, check_vma=False
    )
```

time: 114 us -> 85.9 us (0.75)
  Pallas kernels: 99.9 us -> 77.4 us
  local copies, waits for them, and re-layouts: 10.3 us -> 5.72 us
    pallas_call x5 -> x1, Pallas kernels: 99.9 us -> 77.4 us  [one_step(): pl.pallas_call(functools.partial(step_kernel, spans, devices), out_shape=...]
    reshape x4 -> x0, local copies, waits for them, and re-layouts: 2.13 us -> none  [the longest x2 1.69 us: per_device(): direction.reshape(2, 8, own_patches, PX).transpose(2, 1, 0, 3)]
    unnamed x13 -> x17, local copies, waits for them, and re-layouts: 3.62 us -> 5.38 us
    pallas_call x1 -> x0, local copies, waits for them, and re-layouts: 1.32 us -> none  [gather_up(): pl.pallas_call(gather_up_kernel, out_shape=jax.ShapeDtypeStruct((rows,) +...]
where the time goes in v1:
time: 85.9 us; the launch traced here: 85.5 us
  Pallas kernels  77.4 us (90%)
  local copies, waits for them, and re-layouts  5.72 us (7%)
  other arithmetic  1.65 us (2%)
    pallas_call x1, Pallas kernels, one_step(): pl.pallas_call(functools.partial(step_kernel, spans, devices), out_shape=...  77.4 us
    unnamed x17, local copies, waits for them, and re-layouts  5.38 us

profile of v1, /device:TPU:0, one launch (start us, length us, event | category | flops | bytes accessed | tf_op | source)
XLA Modules:
  0.0 85.5 jit_solution(4368230643630957780)
XLA Ops:
  0.6 0.8 copy.13
  1.4 0.1 reshape.107
  1.5 0.2 convert_reduce_fusion
  1.7 0.1 select_reduce_fusion
  1.8 0.1 reduce_sum.22
  1.9 0.0 copy-start.2
  1.9 0.0 copy-start.5
  2.0 0.0 copy-start.6
  2.0 0.7 copy-done.2
  2.7 0.0 copy-done.5
  2.7 0.0 copy-done.6
  2.7 0.0 copy-start
  2.7 1.0 %copy-done = f32[16,8192]{1,0:T(8,128)S(1)} copy-done((f32[16,8192]{1,0:T(8,128)S(1)}, f32[16,8192]{1,0:T(8,128)}, u32[]{:S(2)}) %copy-start) | copy-done | bytes 524312
  3.7 0.0 copy-start.1
  3.7 1.0 %copy-done.1 = f32[16,8192]{1,0:T(8,128)S(1)} copy-done((f32[16,8192]{1,0:T(8,128)S(1)}, f32[16,8192]{1,0:T(8,128)}, u32[]{:S(2)}) %copy-start.1) | copy-done | bytes 524312
  4.8 0.0 copy-start.3
  4.8 0.9 %copy-done.3 = s32[32,1024]{1,0:T(8,128)S(1)} copy-done((s32[32,1024]{1,0:T(8,128)S(1)}, s32[32,1024]{1,0:T(8,128)}, u32[]{:S(2)}) %copy-start.3) | copy-done | bytes 131096
  5.7 0.0 copy-start.4
  5.7 0.9 %copy-done.4 = f32[32,1024]{1,0:T(8,128)S(1)} copy-done((f32[32,1024]{1,0:T(8,128)S(1)}, f32[32,1024]{1,0:T(8,128)}, u32[]{:S(2)}) %copy-start.4) | copy-done | bytes 131096
  6.6 0.0 copy-start.7
  6.6 77.4 %shard_map.112 = (f32[16,8192]{1,0:T(8,128)S(1)}, f32[16,128]{1,0:T(8,128)S(1)}) custom-call(s32[256]{0:T(256)S(1)} %multiply_add_fusion.2.slot_ref, s32[256]{0:T(256)S(1)} %and_select_fusion.block_ref, f32[32]{0:T(128)S(1)} %copy-done.6, s32[32,1,128]{2,1,0:T(1,128)S(1)} %bitcast.3, f32[16,8192]{1,0:T(8,128)S(1)} %copy-done, f32[16,8192]{1,0:T(8,128)S(1)} %copy-done.1, ...), custom_call_target="tpu_custom_call" | custom-call | tf_op jit(solution)/shard_map/pallas_call | solution.py:399
  84.0 0.2 slice_reduce_fusion
  84.2 0.0 copy-done.7
  84.2 1.3 %multiply_add_fusion = (f32[16,8192]{1,0:T(8,128)}, f32[16,8192]{1,0:T(8,128)}, f32[16,8192]{1,0:T(8,128)}) fusion(f32[16,8192]{1,0:T(8,128)S(1)} %copy-done, f32[16]{0:T(128)S(1)} %get-tuple-element.7, f32[8192]{0:T(1024)S(1)} %copy-done.2, f32[16,8192]{1,0:T(8,128)S(1)} %copy-done.1, f32[16,8192]{1,0:T(8,128)S(1)} %get-tuple-element.6, ...), kind=kLoop, calls=%fused_computation | loop fusion | flops 917504 | bytes 3702912 | tf_op jit(solution)/shard_map/add | solution.py:475
  (5 shorter events, 0.0 us)
Async XLA Ops:
  1.9 0.8 copy-start.2
  1.9 0.7 copy-start.5
  2.0 0.7 copy-start.6
  2.7 1.0 %copy-start = (f32[16,8192]{1,0:T(8,128)S(1)}, f32[16,8192]{1,0:T(8,128)}, u32[]{:S(2)}) copy-start(f32[16,8192]{1,0:T(8,128)} %way_ref.1) | copy-start | bytes 1572868
  3.7 1.0 %copy-start.1 = (f32[16,8192]{1,0:T(8,128)S(1)}, f32[16,8192]{1,0:T(8,128)}, u32[]{:S(2)}) copy-start(f32[16,8192]{1,0:T(8,128)} %old_ref.1) | copy-start | bytes 1572868
  4.8 0.9 %copy-start.3 = (s32[32,1024]{1,0:T(8,128)S(1)}, s32[32,1024]{1,0:T(8,128)}, u32[]{:S(2)}) copy-start(s32[32,1024]{1,0:T(8,128)} %pixel_ref.1) | copy-start | bytes 393220
  5.7 0.9 %copy-start.4 = (f32[32,1024]{1,0:T(8,128)S(1)}, f32[32,1024]{1,0:T(8,128)}, u32[]{:S(2)}) copy-start(f32[32,1024]{1,0:T(8,128)} %gain_ref.1) | copy-start | bytes 393220
  6.6 77.6 %copy-start.7 = (f32[16,8192]{1,0:T(8,128)S(1)}, f32[16,8192]{1,0:T(8,128)}, u32[]{:S(2)}) copy-start(f32[16,8192]{1,0:T(8,128)} %param.9) | copy-start | bytes 1572868

commit v2 on v1

--- a/solution.py
+++ b/solution.py
@@ -1,5 +1,4 @@
 import functools
-import math
 
 import jax
 import jax.numpy as jnp
@@ -17,6 +16,9 @@
     return top, (values - top.astype(jnp.float32)).astype(jnp.bfloat16)
 
 
+PARTS = 4
+
+
 def vmem(count):
     return [pl.BlockSpec(memory_space=pltpu.VMEM)] * count
 
@@ -25,20 +27,15 @@
     return [pl.BlockSpec(memory_space=pltpu.SMEM)] * count
 
 
-def peers_of(spans, devices):
-    me = lax.axis_index("det") * spans + lax.axis_index("tm")
-    stride = spans + 1 if math.gcd(spans + 1, devices) == 1 else 1
-
-    def ahead(step):
-        return lax.rem(me + step * stride, devices)
-
-    def behind(step):
-        return lax.rem(me + (devices - step) * stride, devices)
-
-    def place(peer):
-        return (peer // spans, lax.rem(peer, spans))
-
-    return me, ahead, behind, place
+def partners_of(groups, spans):
+    group, span = lax.axis_index("det"), lax.axis_index("tm")
+    me = group * spans + span
+    shift = spans.bit_length() - 1
+
+    def place(mask):
+        return (group ^ (mask >> shift), span ^ (mask & (spans - 1)))
+
+    return me, group, span, place
 
 
 def remote(src, dst, sent, got, device):
@@ -48,15 +45,17 @@
 
 
 def step_kernel(
-    spans, devices,
-    slot_ref, block_ref, diag_ref, ask_ref, way_ref, old_ref, scale_ref, pixel_ref, gain_ref, band_ref,
+    groups, spans,
+    slot_ref, block_ref, diag_ref, ask_ref, way_hbm, old_hbm, scale_hbm, pixel_hbm, gain_hbm, band_ref,
     image_ref, factor_ref,
-    asked, numbers, table, served, patches, pixels, turned, gains, turned_gains, line, bands, hot,
+    way_ref, old_ref, scale_ref, pixel_ref, gain_ref,
+    numbers, asked, table, served, patches, pixels, turned, gains, turned_gains, line, bands, hot,
     head, tail, before, after, cells, part, collected, spread, image, sums, held,
-    ask_sent, ask_got, sent, got, local, edge_sent, edge_got, back_sent, back_got, sum_sent, sum_got,
+    load_sem, ask_sent, ask_got, local, sent, got, edge_sent, edge_got, back_sent, back_got,
+    sum_sent, sum_got,
 ):
-    me, ahead, behind, place = peers_of(spans, devices)
-    span, group = lax.axis_index("tm"), lax.axis_index("det")
+    devices = groups * spans
+    me, group, span, place = partners_of(groups, spans)
     rows = pixel_ref.shape[0]
     blocks = block_ref.shape[0]
     per_row = blocks // rows
@@ -65,13 +64,32 @@
     half = rows // 2
     tiles = way_ref.shape[1] // 128
     deep = pairs * 8
+    others = devices - 1
+    width = devices // PARTS
     left = lax.broadcasted_iota(jnp.int32, (8, 128), 1) < 64
 
+    loads = [
+        pltpu.make_async_copy(src, dst, load_sem.at[i])
+        for i, (src, dst) in enumerate(
+            [(way_hbm, way_ref), (pixel_hbm, pixel_ref), (gain_hbm, gain_ref), (old_hbm, old_ref), (scale_hbm, scale_ref)]
+        )
+    ]
+    for load in loads:
+        load.start()
+
     barrier = pltpu.get_barrier_semaphore()
 
-    @pl.loop(1, devices)
-    def _(step):
-        pl.semaphore_signal(barrier, inc=1, device_id=place(ahead(step)), device_id_type=MESH)
+    def partners(run):
+        @pl.loop(0, others)
+        def _(n):
+            run(others - n)
+
+    @functools.partial(partners)
+    def _(mask):
+        pl.semaphore_signal(barrier, inc=1, device_id=place(mask), device_id_type=MESH)
+
+    asked[0] = ask_ref[me]
+    loads[0].wait()
 
     @pl.loop(0, tiles, unroll=2)
     def _(q):
@@ -80,26 +98,26 @@
             table[0, h, q] = tile
             table[1, h, q] = pltpu.roll(tile, 64, 1)
 
-    pl.semaphore_wait(barrier, devices - 1)
-
-    def ask(step, slot):
-        peer = ahead(step)
+    pl.semaphore_wait(barrier, others)
+
+    def ask(mask):
+        return remote(ask_ref.at[me ^ mask], asked.at[mask], ask_sent, ask_got, place(mask))
+
+    def give(h, mask):
         return remote(
-            ask_ref.at[peer], asked.at[slot], ask_sent.at[step], ask_got.at[step], place(peer)
+            served.at[h, mask], patches.at[h, mask], sent, got.at[h, mask // width], place(mask)
         )
 
-    def give(h, step, slot):
-        peer = ahead(step)
-        return remote(
-            served.at[h, peer], patches.at[h, slot], sent.at[h, step], got.at[h, step], place(peer)
-        )
-
-    @pl.loop(1, devices)
-    def _(step):
-        ask(step, me).start()
-
-    asked[me] = ask_ref[me]
-
+    def whole(ref, low, high, sent_sem, got_sem):
+        these = ref.at[pl.ds(low, high - low)]
+        return remote(these, these, sent_sem, got_sem, place(1))
+
+    @functools.partial(partners)
+    def _(mask):
+        ask(mask).start()
+
+    loads[1].wait()
+    loads[2].wait()
     for r in range(0, rows, 8):
         for j in range(per_row):
             these = pl.ds(r * per_row + j, 8, stride=per_row)
@@ -110,27 +128,25 @@
             gains[these, :] = gain
             turned_gains[these, :] = pltpu.roll(gain, 64, 1)
 
-    @pl.loop(1, devices)
-    def _(step):
-        ask(step, behind(step)).wait_recv()
-
+    whole(asked, 1, devices, ask_sent, ask_got).wait_recv()
     move = pltpu.make_async_copy(asked, numbers, local)
     move.start()
     move.wait()
 
-    def serve(h, peer, dst):
+    def serve(h, mask, dst):
         for i in range(pairs):
-            a, b = numbers[peer, 0, 2 * i], numbers[peer, 0, 2 * i + 1]
-            dst[h, peer, i] = jnp.where(left, table[a & 1, h, a >> 1], table[1 - (b & 1), h, b >> 1])
+            a, b = numbers[mask, 0, 2 * i], numbers[mask, 0, 2 * i + 1]
+            dst[h, mask, i] = jnp.where(left, table[a & 1, h, a >> 1], table[1 - (b & 1), h, b >> 1])
 
     for h in range(2):
 
-        @pl.loop(1, devices)
-        def _(step):
-            serve(h, ahead(step), served)
-            give(h, step, me).start()
-
-        serve(h, me, patches)
+        @functools.partial(partners)
+        def _(mask):
+            serve(h, mask, served)
+            give(h, mask).start()
+
+        serve(h, 0, patches)
+
 
     lane = lax.broadcasted_iota(jnp.int32, (1, 128), 1)
     band = jnp.concatenate([band_ref[...], jnp.zeros((rows, 128 - band_ref.shape[1]), jnp.float32)], axis=1)
@@ -139,9 +155,7 @@
     lower = jnp.where(
         lane == 0, jnp.take_along_axis(band, jnp.full((rows, 128), 63, jnp.int32), axis=1), 0.0
     )
-    sums[...] = jnp.zeros_like(sums)
-    cells_of_band = jnp.concatenate([lower, upper], axis=1)
-    held_bands = cells_of_band
+    held_bands = jnp.concatenate([lower, upper], axis=1)
 
     wide_lane = lax.broadcasted_iota(jnp.int32, (1, 256), 1)
     for d in range(rows):
@@ -176,21 +190,25 @@
     crossed = jnp.where(jnp.where(first, odd, even) == target, 1.0, 0.0)
     spread[...] = jnp.concatenate([straight.T, crossed.T], axis=1).astype(jnp.bfloat16)
 
-    def scan(h, peer):
+    def scan(h, mask):
         for i in range(pairs):
-            patch = patches[h, peer, i]
+            patch = patches[h, mask, i]
             for side in range(2):
-                s = peer * per_owner + 2 * i + side
+                s = (me ^ mask) * per_owner + 2 * i + side
                 b = block_ref[s]
                 pixel = jnp.broadcast_to(turned[pl.ds(b, 1), :], (8, 128)) + 64 * side
                 gain = jnp.broadcast_to(turned_gains[pl.ds(b, 1), :], (8, 128))
                 line[h, s] = jnp.take_along_axis(patch, pixel, axis=1) * gain
 
-    def arrive(h, low, high):
-        @pl.loop(low, high)
-        def _(step):
-            give(h, step, behind(step)).wait_recv()
-            scan(h, behind(step))
+    def arrive(h):
+        scan(h, 0)
+        for g in reversed(range(PARTS)):
+            low, high = max(1, g * width), (g + 1) * width
+            whole(patches.at[h], low, high, sent, got.at[h, g]).wait_recv()
+
+            @pl.loop(low, high)
+            def _(mask):
+                scan(h, mask)
 
     forth = [
         remote(tail.at[h], before.at[h], edge_sent.at[h, 0], edge_got.at[h, 0],
@@ -256,9 +274,9 @@
 
     blank = jnp.zeros((PX, 128), jnp.bfloat16)
 
-    def project(h, peer, dst, where):
+    def project(h, mask, dst):
         for i in range(pairs):
-            s = peer * per_owner + 2 * i
+            s = (me ^ mask) * per_owner + 2 * i
             both = jnp.concatenate([cells[h, block_ref[s]], cells[h, block_ref[s + 1]]], axis=1)
             grid = jnp.concatenate(
                 [
@@ -270,31 +288,31 @@
             added = lax.dot_general(
                 both, grid, (((1,), (1,)), ((), ())), preferred_element_type=jnp.float32
             )
-            dst[pl.ds(pl.multiple_of(where + 8 * i, 8), 8), :] = added[:8] + added[8:]
-
-    def rows_of(h, slot):
-        return pl.ds(pl.multiple_of((h * devices + slot) * deep, 8), deep)
-
-    def send_back(h, step, slot):
-        peer = ahead(step)
+            where = (h * devices + mask) * deep + 8 * i
+            dst[pl.ds(pl.multiple_of(where, 8), 8), :] = added[:8] + added[8:]
+
+    def rows_of(h, mask, count):
+        return pl.ds(pl.multiple_of((h * devices + mask) * deep, 8), count * deep)
+
+    def send_back(h, mask):
+        these = rows_of(h, mask, 1)
         return remote(
-            part.at[rows_of(h, peer)], collected.at[rows_of(h, slot)],
-            back_sent.at[h, step], back_got.at[h, step], place(peer),
+            part.at[these], collected.at[these], back_sent, back_got.at[h, mask // width], place(mask)
         )
 
     def project_all(h):
-        @pl.loop(1, devices)
-        def _(step):
-            peer = ahead(step)
-            project(h, peer, part, (h * devices + peer) * deep)
-            send_back(h, step, me).start()
-
-        project(h, me, collected, (h * devices + me) * deep)
+        @functools.partial(partners)
+        def _(mask):
+            project(h, mask, part)
+            send_back(h, mask).start()
+
+        project(h, 0, collected)
 
     def gather_up(h):
-        @pl.loop(1, devices)
-        def _(step):
-            send_back(h, step, behind(step)).wait_recv()
+        for g in reversed(range(PARTS)):
+            low, high = max(1, g * width), (g + 1) * width
+            these = collected.at[rows_of(h, low, high - low)]
+            remote(these, these, back_sent, back_got.at[h, g], place(1)).wait_recv()
 
         wide_left = lax.broadcasted_iota(jnp.int32, (tiles, 128), 1) < 64
         for k in range(8):
@@ -331,82 +349,83 @@
                 totals[3] + tile * (scale * tile),
             )
 
-        totals = lax.fori_loop(0, tiles, add, (zero,) * 4, unroll=4)
-        whole = sums[...]
-        lanes = lax.broadcasted_iota(jnp.int32, (8, 128), 1)
-        for i, total in enumerate(totals):
-            whole = jnp.where(lanes == 4 * h + i, jnp.sum(total, axis=1, keepdims=True), whole)
-        sums[...] = whole
-
-    scan(0, me)
-    arrive(0, 1, devices)
+        return [
+            jnp.sum(total, axis=1, keepdims=True)
+            for total in lax.fori_loop(0, tiles, add, (zero,) * 4, unroll=4)
+        ]
+
+    arrive(0)
     edges(0)
-    scan(1, me)
-    arrive(1, 1, devices // 2)
     edges_in(0)
     filter_all(0)
-    arrive(1, devices // 2, devices)
+    project_all(0)
+    arrive(1)
     edges(1)
-    project_all(0)
     edges_in(1)
     filter_all(1)
     project_all(1)
-
-    @pl.loop(1, devices)
-    def _(step):
-        ask(step, me).wait_send()
-        give(0, step, me).wait_send()
-        give(1, step, me).wait_send()
-
-    gather_up(0)
-    gather_up(1)
-
-    def give_sums(step, slot):
-        return remote(sums, held.at[slot], sum_sent.at[step], sum_got.at[step], place(ahead(step)))
-
-    @pl.loop(1, devices)
-    def _(step):
-        give_sums(step, me).start()
-
-    held[me] = sums[...]
-
-    @pl.loop(1, devices)
-    def _(step):
-        send_back(0, step, me).wait_send()
-        send_back(1, step, me).wait_send()
-        give_sums(step, me).wait_send()
-        give_sums(step, behind(step)).wait_recv()
-
-    total = jnp.sum(held[...], axis=0)
+    whole(ask_ref, 1, devices, ask_sent, ask_got).wait_send()
     for h in range(2):
-        norm_old, curvature, cross, square = (total[:, 4 * h + i : 4 * h + i + 1] for i in range(4))
+        whole(served.at[h], 1, devices, sent, sent).wait_send()
+    loads[3].wait()
+    loads[4].wait()
+
+    lanes = lax.broadcasted_iota(jnp.int32, (8, 128), 1)
+    places = lax.broadcasted_iota(jnp.int32, (8, 128), 0)
+    row = jnp.zeros((8, 128), jnp.float32)
+    for h in range(2):
+        for i, total in enumerate(gather_up(h)):
+            row = jnp.where(lanes == places * 8 + 4 * h + i, total, row)
+    sums[...] = jnp.sum(row, axis=0, keepdims=True)
+
+    def give_sums(mask):
+        return remote(sums, held.at[mask], sum_sent, sum_got, place(mask))
+
+    @functools.partial(partners)
+    def _(mask):
+        give_sums(mask).start()
+
+    held[0] = sums[...]
+    for h in range(2):
+        these = part.at[rows_of(h, 1, others)]
+        remote(these, these, back_sent, back_sent, place(1)).wait_send()
+    whole(held, 1, devices, sum_sent, sum_got).wait()
+    total = jnp.broadcast_to(jnp.sum(held[...], axis=0), (8, 128))
+    for h in range(2):
+        norm_old, curvature, cross, square = (
+            jnp.take_along_axis(total, places * 8 + 4 * h + i, axis=1) for i in range(4)
+        )
         step_size = norm_old / curvature
         norm_new = norm_old - step_size * (2.0 * cross - step_size * square)
-        lanes = lax.broadcasted_iota(jnp.int32, (8, 128), 1)
         factor_ref[8 * h : 8 * h + 8, :] = jnp.where(lanes == 0, step_size, norm_new / norm_old)
 
 
-def one_step(slot, block, diag, ask, way, old, scale, pixels, gains, band, spans, devices):
+def one_step(slot, block, diag, ask, way, old, scale, pixels, gains, band, groups, spans):
+    devices = groups * spans
     blocks = slot.shape[0]
     rows = pixels.shape[0]
-    per_owner = blocks // devices
-    pairs = per_owner // 2
+    pairs = blocks // devices // 2
     tiles = way.shape[1] // 128
     edge = (2, rows // 2, 8, 128)
     both = (2, devices, pairs, 8, 128)
     flat = (2 * devices * pairs * 8, 128)
     dma = pltpu.SemaphoreType.DMA
     return pl.pallas_call(
-        functools.partial(step_kernel, spans, devices),
+        functools.partial(step_kernel, groups, spans),
         out_shape=(
             jax.ShapeDtypeStruct(way.shape, jnp.float32),
             jax.ShapeDtypeStruct((way.shape[0], 128), jnp.float32),
         ),
-        in_specs=smem(3) + vmem(7),
+        in_specs=smem(3) + vmem(1) + [pl.BlockSpec(memory_space=pltpu.HBM)] * 5 + vmem(1),
         out_specs=tuple(vmem(2)),
         scratch_shapes=[
+            pltpu.VMEM(way.shape, jnp.float32),
+            pltpu.VMEM(old.shape, jnp.float32),
+            pltpu.VMEM(scale.shape, jnp.float32),
+            pltpu.VMEM(pixels.shape, jnp.int32),
+            pltpu.VMEM(gains.shape, jnp.float32),
+            pltpu.SMEM(ask.shape, jnp.int32),
             pltpu.VMEM(ask.shape, jnp.int32),
-            pltpu.SMEM(ask.shape, jnp.int32),
             pltpu.VMEM((2, 2, tiles, 8, 128), jnp.float32),
             pltpu.VMEM(both, jnp.float32),
             pltpu.VMEM(both, jnp.float32),
@@ -426,19 +445,20 @@
             pltpu.VMEM(flat, jnp.float32),
             pltpu.VMEM((2 * tiles, blocks), jnp.bfloat16),
             pltpu.VMEM((2 * tiles * 8, 128), jnp.float32),
-            pltpu.VMEM((8, 128), jnp.float32),
-            pltpu.VMEM((devices, 8, 128), jnp.float32),
-            dma((devices,)),
-            dma((devices,)),
-            dma((2, devices)),
-            dma((2, devices)),
-            dma,
+            pltpu.VMEM((1, 128), jnp.float32),
+            pltpu.VMEM((devices, 1, 128), jnp.float32),
+            dma((5,)),
+            dma,
+            dma,
+            dma,
+            dma,
+            dma((2, PARTS)),
             dma((2, 2)),
             dma((2, 2)),
-            dma((2, devices)),
-            dma((2, devices)),
-            dma((devices,)),
-            dma((devices,)),
+            dma,
+            dma((2, PARTS)),
+            dma,
+            dma,
         ],
         compiler_params=pltpu.CompilerParams(
             collective_id=0, has_side_effects=True, vmem_limit_bytes=48 * 1024 * 1024
@@ -450,8 +470,8 @@
     iterate, residual, direction, precond, patch_ids, pixel_in, weights, filter_diag, filter_band
 ):
     det_rows, time_blocks = patch_ids.shape
-    spans = lax.axis_size("tm")
-    devices = lax.axis_size("det") * spans
+    groups, spans = lax.axis_size("det"), lax.axis_size("tm")
+    devices = groups * spans
     blocks = det_rows * time_blocks
     per_owner = blocks // devices
     own_patches = iterate.shape[1] // PX
@@ -467,7 +487,7 @@
     requests = jnp.pad(requests, ((0, 0), (0, 128 - per_owner)))[:, None, :]
     image_map, factor = one_step(
         slot, block, filter_diag, requests, direction, residual, precond[None, :],
-        pixel_in, weights, filter_band, spans, devices,
+        pixel_in, weights, filter_band, groups, spans,
     )
     step_size, ratio = factor[:, 0:1], factor[:, 1:2]
     new_iterate = iterate + step_size * direction

time: 85.9 us -> 83.5 us (0.972)
  Pallas kernels: 77.4 us -> 75.1 us
    pallas_call x1, Pallas kernels: 77.4 us -> 75.1 us  [one_step(): pl.pallas_call(functools.partial(step_kernel, groups, spans), out_shape=(...]
where the time goes in v2:
time: 83.5 us; the launch traced here: 83.1 us
  Pallas kernels  75.1 us (90%)
  local copies, waits for them, and re-layouts  5.72 us (7%)
  other arithmetic  1.65 us (2%)
    pallas_call x1, Pallas kernels, one_step(): pl.pallas_call(functools.partial(step_kernel, groups, spans), out_shape=(...  75.1 us
    unnamed x17, local copies, waits for them, and re-layouts  5.38 us

profile of v2, /device:TPU:0, one launch (start us, length us, event | category | flops | bytes accessed | tf_op | source)
XLA Modules:
  0.0 83.1 jit_solution(16544904926406096316)
XLA Ops:
  0.6 0.8 copy.13
  1.4 0.1 reshape.107
  1.5 0.2 convert_reduce_fusion
  1.7 0.1 select_reduce_fusion
  1.8 0.1 reduce_sum.22
  1.9 0.0 copy-start.2
  1.9 0.0 copy-start.5
  2.0 0.0 copy-start.6
  2.0 0.7 copy-done.2
  2.7 0.0 copy-done.5
  2.7 0.0 copy-done.6
  2.7 0.0 copy-start
  2.7 1.0 %copy-done = f32[16,8192]{1,0:T(8,128)S(1)} copy-done((f32[16,8192]{1,0:T(8,128)S(1)}, f32[16,8192]{1,0:T(8,128)}, u32[]{:S(2)}) %copy-start) | copy-done | bytes 524312
  3.7 0.0 copy-start.1
  3.7 1.0 %copy-done.1 = f32[16,8192]{1,0:T(8,128)S(1)} copy-done((f32[16,8192]{1,0:T(8,128)S(1)}, f32[16,8192]{1,0:T(8,128)}, u32[]{:S(2)}) %copy-start.1) | copy-done | bytes 524312
  4.8 0.0 copy-start.3
  4.8 0.9 %copy-done.3 = s32[32,1024]{1,0:T(8,128)S(1)} copy-done((s32[32,1024]{1,0:T(8,128)S(1)}, s32[32,1024]{1,0:T(8,128)}, u32[]{:S(2)}) %copy-start.3) | copy-done | bytes 131096
  5.7 0.0 copy-start.4
  5.7 0.9 %copy-done.4 = f32[32,1024]{1,0:T(8,128)S(1)} copy-done((f32[32,1024]{1,0:T(8,128)S(1)}, f32[32,1024]{1,0:T(8,128)}, u32[]{:S(2)}) %copy-start.4) | copy-done | bytes 131096
  6.6 0.0 copy-start.7
  6.6 75.1 %shard_map.112 = (f32[16,8192]{1,0:T(8,128)S(1)}, f32[16,128]{1,0:T(8,128)S(1)}) custom-call(s32[256]{0:T(256)S(1)} %multiply_add_fusion.2.slot_ref, s32[256]{0:T(256)S(1)} %and_select_fusion.block_ref, f32[32]{0:T(128)S(1)} %copy-done.6, s32[32,1,128]{2,1,0:T(1,128)S(1)} %bitcast.3, f32[16,8192]{1,0:T(8,128)S(1)} %copy-done, f32[16,8192]{1,0:T(8,128)S(1)} %copy-done.1, ...), custom_call_target="tpu_custom_call" | custom-call | tf_op jit(solution)/shard_map/pallas_call | solution.py:413
  81.6 0.2 slice_reduce_fusion
  81.8 0.0 copy-done.7
  81.8 1.3 %multiply_add_fusion = (f32[16,8192]{1,0:T(8,128)}, f32[16,8192]{1,0:T(8,128)}, f32[16,8192]{1,0:T(8,128)}) fusion(f32[16,8192]{1,0:T(8,128)S(1)} %copy-done, f32[16]{0:T(128)S(1)} %get-tuple-element.7, f32[8192]{0:T(1024)S(1)} %copy-done.2, f32[16,8192]{1,0:T(8,128)S(1)} %copy-done.1, f32[16,8192]{1,0:T(8,128)S(1)} %get-tuple-element.6, ...), kind=kLoop, calls=%fused_computation | loop fusion | flops 917504 | bytes 3702912 | tf_op jit(solution)/shard_map/add | solution.py:495
  (5 shorter events, 0.0 us)
Async XLA Ops:
  1.9 0.8 copy-start.2
  1.9 0.7 copy-start.5
  2.0 0.7 copy-start.6
  2.7 1.0 %copy-start = (f32[16,8192]{1,0:T(8,128)S(1)}, f32[16,8192]{1,0:T(8,128)}, u32[]{:S(2)}) copy-start(f32[16,8192]{1,0:T(8,128)} %way_hbm.1) | copy-start | bytes 1572868
  3.7 1.0 %copy-start.1 = (f32[16,8192]{1,0:T(8,128)S(1)}, f32[16,8192]{1,0:T(8,128)}, u32[]{:S(2)}) copy-start(f32[16,8192]{1,0:T(8,128)} %old_hbm.1) | copy-start | bytes 1572868
  4.8 0.9 %copy-start.3 = (s32[32,1024]{1,0:T(8,128)S(1)}, s32[32,1024]{1,0:T(8,128)}, u32[]{:S(2)}) copy-start(s32[32,1024]{1,0:T(8,128)} %pixel_hbm.1) | copy-start | bytes 393220
  5.7 0.9 %copy-start.4 = (f32[32,1024]{1,0:T(8,128)S(1)}, f32[32,1024]{1,0:T(8,128)}, u32[]{:S(2)}) copy-start(f32[32,1024]{1,0:T(8,128)} %gain_hbm.1) | copy-start | bytes 393220
  6.6 75.2 %copy-start.7 = (f32[16,8192]{1,0:T(8,128)S(1)}, f32[16,8192]{1,0:T(8,128)}, u32[]{:S(2)}) copy-start(f32[16,8192]{1,0:T(8,128)} %param.9) | copy-start | bytes 1572868

commit v3 on v2

--- a/solution.py
+++ b/solution.py
@@ -46,18 +46,18 @@
 
 def step_kernel(
     groups, spans,
-    slot_ref, block_ref, diag_ref, ask_ref, way_hbm, old_hbm, scale_hbm, pixel_hbm, gain_hbm, band_ref,
+    diag_ref, patch_ref, way_hbm, old_hbm, scale_hbm, pixel_hbm, gain_hbm, band_ref,
     image_ref, factor_ref,
     way_ref, old_ref, scale_ref, pixel_ref, gain_ref,
-    numbers, asked, table, served, patches, pixels, turned, gains, turned_gains, line, bands, hot,
+    slot_ref, block_ref, slots, listed, ask_ref, numbers, asked, table, served, patches, pixels, turned, gains, turned_gains, line, bands, hot,
     head, tail, before, after, cells, part, collected, spread, image, sums, held,
-    load_sem, ask_sent, ask_got, local, sent, got, edge_sent, edge_got, back_sent, back_got,
+    load_sem, ask_sent, ask_got, local, list_sem, sent, got, edge_sent, edge_got, back_sent, back_got,
     sum_sent, sum_got,
 ):
     devices = groups * spans
     me, group, span, place = partners_of(groups, spans)
     rows = pixel_ref.shape[0]
-    blocks = block_ref.shape[0]
+    blocks = block_ref.shape[1]
     per_row = blocks // rows
     per_owner = blocks // devices
     pairs = per_owner // 2
@@ -74,9 +74,6 @@
             [(way_hbm, way_ref), (pixel_hbm, pixel_ref), (gain_hbm, gain_ref), (old_hbm, old_ref), (scale_hbm, scale_ref)]
         )
     ]
-    for load in loads:
-        load.start()
-
     barrier = pltpu.get_barrier_semaphore()
 
     def partners(run):
@@ -88,6 +85,63 @@
     def _(mask):
         pl.semaphore_signal(barrier, inc=1, device_id=place(mask), device_id_type=MESH)
 
+    for load in loads:
+        load.start()
+
+    lane8 = lax.broadcasted_iota(jnp.int32, (8, 128), 1)
+    row8 = lax.broadcasted_iota(jnp.int32, (8, 128), 0)
+    lane1 = lax.broadcasted_iota(jnp.int32, (1, 128), 1)
+    square_row = lax.broadcasted_iota(jnp.int32, (128, 128), 0)
+    square_lane = lax.broadcasted_iota(jnp.int32, (128, 128), 1)
+    own_patches = 2 * tiles
+    own_shift = own_patches.bit_length() - 1
+    row_shift = rows.bit_length() - 1
+    chunks = range(blocks // 128)
+
+    def as_column(row):
+        return jnp.broadcast_to(row, (128, 128)).T
+
+    def down(values):
+        return jnp.sum(values, axis=0, keepdims=True)
+
+    padded = jnp.concatenate([patch_ref[...], jnp.zeros((per_row, 128 - rows), jnp.int32)], axis=1)
+    repeated = jnp.take_along_axis(padded, lane8 & (rows - 1), axis=1)
+    lies = [
+        down(jnp.where(row8 == k * (128 // rows) + (lane8 >> row_shift), repeated, 0)) for k in chunks
+    ]
+    owners = [jnp.right_shift(lie, own_shift) for lie in lies]
+    packed = [
+        (((lane1 & (rows - 1)) * per_row + k * (128 // rows) + (lane1 >> row_shift)) << own_shift)
+        + (lies[k] & (own_patches - 1))
+        for k in chunks
+    ]
+    owner_columns = [as_column(owner) for owner in owners]
+    packed_columns = [as_column(pack) for pack in packed]
+    slot_rows = []
+    for k in chunks:
+        rank = jnp.zeros((128, 128), jnp.int32)
+        for c in chunks:
+            same = (owner_columns[c] == owners[k]) & (square_row + 128 * c < square_lane + 128 * k)
+            rank = rank + jnp.where(same, 1, 0)
+        slot_rows.append(owners[k] * per_owner + down(rank))
+        slots[:, 128 * k : 128 * k + 128] = slot_rows[k] & (blocks - 1)
+    slot_columns = [as_column(row) for row in slot_rows]
+    for k in chunks:
+        found = jnp.zeros((128, 128), jnp.int32)
+        for c in chunks:
+            found = found + jnp.where(slot_columns[c] == square_lane + 128 * k, packed_columns[c], 0)
+        by_slot = down(found)
+        listed[:, 128 * k : 128 * k + 128] = jnp.right_shift(by_slot, own_shift) & (blocks - 1)
+        wide = jnp.broadcast_to(by_slot & (own_patches - 1), (8, 128))
+        for p in range(128 // per_owner):
+            turn = (128 - p * per_owner) % 128
+            ask_ref[k * (128 // per_owner) + p] = (pltpu.roll(wide, turn, 1) if turn else wide)[:1]
+    lists = [
+        pltpu.make_async_copy(slots, slot_ref, list_sem.at[0]),
+        pltpu.make_async_copy(listed, block_ref, list_sem.at[1]),
+    ]
+    for copy in lists:
+        copy.start()
     asked[0] = ask_ref[me]
     loads[0].wait()
 
@@ -115,6 +169,32 @@
     @functools.partial(partners)
     def _(mask):
         ask(mask).start()
+
+    whole(asked, 1, devices, ask_sent, ask_got).wait_recv()
+    move = pltpu.make_async_copy(asked, numbers, local)
+    move.start()
+    move.wait()
+
+    def serve(h, mask, dst):
+        for i in range(pairs):
+            a, b = numbers[mask, 0, 2 * i], numbers[mask, 0, 2 * i + 1]
+            dst[h, mask, i] = jnp.where(left, table[a & 1, h, a >> 1], table[1 - (b & 1), h, b >> 1])
+
+    def part_of(g):
+        return max(1, g * width), (g + 1) * width
+
+    def offer(h, g):
+        low, high = part_of(g)
+
+        @pl.loop(low, high)
+        def _(mask):
+            serve(h, mask, served)
+            give(h, mask).start()
+
+    for g in reversed(range(PARTS)):
+        offer(0, g)
+    for h in range(2):
+        serve(h, 0, patches)
 
     loads[1].wait()
     loads[2].wait()
@@ -128,25 +208,8 @@
             gains[these, :] = gain
             turned_gains[these, :] = pltpu.roll(gain, 64, 1)
 
-    whole(asked, 1, devices, ask_sent, ask_got).wait_recv()
-    move = pltpu.make_async_copy(asked, numbers, local)
-    move.start()
-    move.wait()
-
-    def serve(h, mask, dst):
-        for i in range(pairs):
-            a, b = numbers[mask, 0, 2 * i], numbers[mask, 0, 2 * i + 1]
-            dst[h, mask, i] = jnp.where(left, table[a & 1, h, a >> 1], table[1 - (b & 1), h, b >> 1])
-
-    for h in range(2):
-
-        @functools.partial(partners)
-        def _(mask):
-            serve(h, mask, served)
-            give(h, mask).start()
-
-        serve(h, 0, patches)
-
+    for copy in lists:
+        copy.wait()
 
     lane = lax.broadcasted_iota(jnp.int32, (1, 128), 1)
     band = jnp.concatenate([band_ref[...], jnp.zeros((rows, 128 - band_ref.shape[1]), jnp.float32)], axis=1)
@@ -173,7 +236,7 @@
 
     @pl.loop(0, blocks, unroll=2)
     def _(s):
-        pixel = jnp.broadcast_to(pixels[pl.ds(block_ref[s], 1), :], (PX, 128))
+        pixel = jnp.broadcast_to(pixels[pl.ds(block_ref[0, s], 1), :], (PX, 128))
         hot[s] = jnp.where(spot == pixel, 1.0, 0.0).astype(jnp.bfloat16)
 
     asks = asked[:, 0, :]
@@ -195,7 +258,7 @@
             patch = patches[h, mask, i]
             for side in range(2):
                 s = (me ^ mask) * per_owner + 2 * i + side
-                b = block_ref[s]
+                b = block_ref[0, s]
                 pixel = jnp.broadcast_to(turned[pl.ds(b, 1), :], (8, 128)) + 64 * side
                 gain = jnp.broadcast_to(turned_gains[pl.ds(b, 1), :], (8, 128))
                 line[h, s] = jnp.take_along_axis(patch, pixel, axis=1) * gain
@@ -203,12 +266,19 @@
     def arrive(h):
         scan(h, 0)
         for g in reversed(range(PARTS)):
-            low, high = max(1, g * width), (g + 1) * width
+            low, high = part_of(g)
             whole(patches.at[h], low, high, sent, got.at[h, g]).wait_recv()
+            if h == 0 and g == PARTS // 2:
+                for later in reversed(range(g, PARTS)):
+                    offer(1, later)
 
             @pl.loop(low, high)
             def _(mask):
                 scan(h, mask)
+
+        if h == 0:
+            for later in reversed(range(PARTS // 2)):
+                offer(1, later)
 
     forth = [
         remote(tail.at[h], before.at[h], edge_sent.at[h, 0], edge_got.at[h, 0],
@@ -224,13 +294,12 @@
     def edges(h):
         @pl.loop(0, half)
         def _(d):
-            start, end = d * per_row, d * per_row + per_row - 1
-            far = half * per_row
+            start, end = d, d + (per_row - 1) * rows
             head[h, d] = jnp.where(
-                left, pltpu.roll(line[h, slot_ref[start]], 64, 1), line[h, slot_ref[start + far]]
+                left, pltpu.roll(line[h, slot_ref[0, start]], 64, 1), line[h, slot_ref[0, start + half]]
             )
             tail[h, d] = jnp.where(
-                left, line[h, slot_ref[end]], pltpu.roll(line[h, slot_ref[end + far]], 64, 1)
+                left, line[h, slot_ref[0, end]], pltpu.roll(line[h, slot_ref[0, end + half]], 64, 1)
             )
 
         forth[h].start()
@@ -249,7 +318,7 @@
             after[h] = jnp.zeros_like(after[h])
 
     def one_row(h, d, early, late):
-        mine = [early] + [line[h, slot_ref[d * per_row + j]] for j in range(per_row)] + [late]
+        mine = [early] + [line[h, slot_ref[0, j * rows + d]] for j in range(per_row)] + [late]
         shifted = [jnp.where(left, mine[m], mine[m + 1]) for m in range(per_row + 1)]
         near = jnp.concatenate(shifted[:-1], axis=0)
         far = jnp.concatenate(shifted[1:], axis=0)
@@ -277,7 +346,7 @@
     def project(h, mask, dst):
         for i in range(pairs):
             s = (me ^ mask) * per_owner + 2 * i
-            both = jnp.concatenate([cells[h, block_ref[s]], cells[h, block_ref[s + 1]]], axis=1)
+            both = jnp.concatenate([cells[h, block_ref[0, s]], cells[h, block_ref[0, s + 1]]], axis=1)
             grid = jnp.concatenate(
                 [
                     jnp.concatenate([hot[s], blank], axis=1),
@@ -300,17 +369,20 @@
             part.at[these], collected.at[these], back_sent, back_got.at[h, mask // width], place(mask)
         )
 
-    def project_all(h):
-        @functools.partial(partners)
+    def project_part(h, g):
+        low, high = part_of(g)
+
+        @pl.loop(low, high)
         def _(mask):
             project(h, mask, part)
             send_back(h, mask).start()
 
-        project(h, 0, collected)
+        if g == 0:
+            project(h, 0, collected)
 
     def gather_up(h):
         for g in reversed(range(PARTS)):
-            low, high = max(1, g * width), (g + 1) * width
+            low, high = part_of(g)
             these = collected.at[rows_of(h, low, high - low)]
             remote(these, these, back_sent, back_got.at[h, g], place(1)).wait_recv()
 
@@ -358,12 +430,16 @@
     edges(0)
     edges_in(0)
     filter_all(0)
-    project_all(0)
+    for g in reversed(range(PARTS // 2, PARTS)):
+        project_part(0, g)
     arrive(1)
     edges(1)
+    for g in reversed(range(PARTS // 2)):
+        project_part(0, g)
     edges_in(1)
     filter_all(1)
-    project_all(1)
+    for g in reversed(range(PARTS)):
+        project_part(1, g)
     whole(ask_ref, 1, devices, ask_sent, ask_got).wait_send()
     for h in range(2):
         whole(served.at[h], 1, devices, sent, sent).wait_send()
@@ -400,15 +476,16 @@
         factor_ref[8 * h : 8 * h + 8, :] = jnp.where(lanes == 0, step_size, norm_new / norm_old)
 
 
-def one_step(slot, block, diag, ask, way, old, scale, pixels, gains, band, groups, spans):
+def one_step(diag, patch, way, old, scale, pixels, gains, band, groups, spans):
     devices = groups * spans
-    blocks = slot.shape[0]
     rows = pixels.shape[0]
+    blocks = patch.size
     pairs = blocks // devices // 2
     tiles = way.shape[1] // 128
     edge = (2, rows // 2, 8, 128)
     both = (2, devices, pairs, 8, 128)
     flat = (2 * devices * pairs * 8, 128)
+    asks = (devices, 1, 128)
     dma = pltpu.SemaphoreType.DMA
     return pl.pallas_call(
         functools.partial(step_kernel, groups, spans),
@@ -416,7 +493,7 @@
             jax.ShapeDtypeStruct(way.shape, jnp.float32),
             jax.ShapeDtypeStruct((way.shape[0], 128), jnp.float32),
         ),
-        in_specs=smem(3) + vmem(1) + [pl.BlockSpec(memory_space=pltpu.HBM)] * 5 + vmem(1),
+        in_specs=smem(1) + vmem(1) + [pl.BlockSpec(memory_space=pltpu.HBM)] * 5 + vmem(1),
         out_specs=tuple(vmem(2)),
         scratch_shapes=[
             pltpu.VMEM(way.shape, jnp.float32),
@@ -424,8 +501,13 @@
             pltpu.VMEM(scale.shape, jnp.float32),
             pltpu.VMEM(pixels.shape, jnp.int32),
             pltpu.VMEM(gains.shape, jnp.float32),
-            pltpu.SMEM(ask.shape, jnp.int32),
-            pltpu.VMEM(ask.shape, jnp.int32),
+            pltpu.SMEM((1, blocks), jnp.int32),
+            pltpu.SMEM((1, blocks), jnp.int32),
+            pltpu.VMEM((1, blocks), jnp.int32),
+            pltpu.VMEM((1, blocks), jnp.int32),
+            pltpu.VMEM(asks, jnp.int32),
+            pltpu.SMEM(asks, jnp.int32),
+            pltpu.VMEM(asks, jnp.int32),
             pltpu.VMEM((2, 2, tiles, 8, 128), jnp.float32),
             pltpu.VMEM(both, jnp.float32),
             pltpu.VMEM(both, jnp.float32),
@@ -451,6 +533,7 @@
             dma,
             dma,
             dma,
+            dma((2,)),
             dma,
             dma((2, PARTS)),
             dma((2, 2)),
@@ -461,32 +544,17 @@
             dma,
         ],
         compiler_params=pltpu.CompilerParams(
-            collective_id=0, has_side_effects=True, vmem_limit_bytes=48 * 1024 * 1024
+            collective_id=0, has_side_effects=True, vmem_limit_bytes=62 * 1024 * 1024
         ),
-    )(slot, block, diag, ask, way, old, scale, pixels, gains, band)
+    )(diag, patch, way, old, scale, pixels, gains, band)
 
 
 def per_device(
     iterate, residual, direction, precond, patch_ids, pixel_in, weights, filter_diag, filter_band
 ):
-    det_rows, time_blocks = patch_ids.shape
     groups, spans = lax.axis_size("det"), lax.axis_size("tm")
-    devices = groups * spans
-    blocks = det_rows * time_blocks
-    per_owner = blocks // devices
-    own_patches = iterate.shape[1] // PX
-    patch_flat = patch_ids.reshape(blocks)
-    owners = patch_flat // own_patches
-    numbers = jnp.arange(blocks, dtype=jnp.int32)
-    earlier = (owners[:, None] == owners[None, :]) & (numbers[None, :] < numbers[:, None])
-    slot = owners * per_owner + jnp.sum(earlier.astype(jnp.int32), axis=1)
-    packed = numbers * own_patches + patch_flat % own_patches
-    by_slot = jnp.sum(jnp.where(numbers[:, None] == slot[None, :], packed[None, :], 0), axis=1)
-    block = by_slot // own_patches
-    requests = (by_slot % own_patches).reshape(devices, per_owner)
-    requests = jnp.pad(requests, ((0, 0), (0, 128 - per_owner)))[:, None, :]
     image_map, factor = one_step(
-        slot, block, filter_diag, requests, direction, residual, precond[None, :],
+        filter_diag, patch_ids.T, direction, residual, precond[None, :],
         pixel_in, weights, filter_band, groups, spans,
     )
     step_size, ratio = factor[:, 0:1], factor[:, 1:2]

time: 83.5 us -> 77.8 us (0.932)
  local copies, waits for them, and re-layouts: 5.72 us -> 0.97 us
  Pallas kernels: 75.1 us -> 73.3 us
  other arithmetic: 1.65 us -> 2.5 us
    unnamed x17 -> x6, local copies, waits for them, and re-layouts: 5.38 us -> 0.01 us
    pallas_call x1, Pallas kernels: 75.1 us -> 73.3 us  [one_step(): pl.pallas_call(functools.partial(step_kernel, groups, spans), out_shape=(...]
    add x1, other arithmetic: 1.31 us -> 2.5 us  [per_device(): new_direction = precond * new_residual + ratio * direction]
where the time goes in v3:
time: 77.8 us; the launch traced here: 77.4 us
  Pallas kernels  73.3 us (94%)
  other arithmetic  2.5 us (3%)
  local copies, waits for them, and re-layouts  0.97 us (1%)
    pallas_call x1, Pallas kernels, one_step(): pl.pallas_call(functools.partial(step_kernel, groups, spans), out_shape=(...  73.3 us
    add x1, other arithmetic, per_device(): new_direction = precond * new_residual + ratio * direction  2.5 us

profile of v3, /device:TPU:0, one launch (start us, length us, event | category | flops | bytes accessed | tf_op | source)
XLA Modules:
  0.0 77.4 jit_solution(14354254089180112149)
XLA Ops:
  0.6 0.0 copy-start
  0.6 0.0 copy-start.1
  0.7 0.0 copy-start.2
  0.7 73.3 %shard_map.112 = (f32[16,8192]{1,0:T(8,128)}, f32[16,128]{1,0:T(8,128)}) custom-call(f32[32]{0:T(128)} %diag_ref.1, s32[8,32]{1,0:T(8,128)} %bitcast.3, f32[16,8192]{1,0:T(8,128)} %way_hbm.1, f32[16,8192]{1,0:T(8,128)} %old_hbm.1, f32[1,8192]{1,0:T(1,128)} %bitcast.2, s32[32,1024]{1,0:T(8,128)} %pixel_hbm.1, f32[32,1024]{1,0:T(8,128)} %gain_hbm.1, ...), custom_call_target="tpu_custom_call" | custom-call | tf_op jit(solution)/shard_map/pallas_call | solution.py:490
  73.9 1.0 %slice_reduce_fusion = (f32[16]{0:T(128)S(1)}, f32[16]{0:T(128)S(1)}) fusion(f32[16,128]{1,0:T(8,128)} %get-tuple-element.5), kind=kLoop, calls=%fused_computation.3 | loop fusion | bytes 256 | tf_op jit(solution)/shard_map/slice | solution.py:560
  74.9 0.0 copy-done
  74.9 0.0 copy-done.1
  74.9 0.0 copy-done.2
  74.9 2.5 %multiply_add_fusion = (f32[16,8192]{1,0:T(8,128)}, f32[16,8192]{1,0:T(8,128)}, f32[16,8192]{1,0:T(8,128)}) fusion(f32[16,8192]{1,0:T(8,128)S(1)} %copy-done, f32[16]{0:T(128)S(1)} %get-tuple-element.7, f32[8192]{0:T(1024)S(1)} %copy-done.2, f32[16,8192]{1,0:T(8,128)S(1)} %copy-done.1, f32[16,8192]{1,0:T(8,128)} %get-tuple-element.6, ...), kind=kLoop, calls=%fused_computation | loop fusion | flops 917504 | bytes 3702912 | tf_op jit(solution)/shard_map/add | solution.py:563
Async XLA Ops:
  0.6 74.3 %copy-start = (f32[16,8192]{1,0:T(8,128)S(1)}, f32[16,8192]{1,0:T(8,128)}, u32[]{:S(2)}) copy-start(f32[16,8192]{1,0:T(8,128)} %way_hbm.1) | copy-start | bytes 1572868
  0.6 74.3 %copy-start.1 = (f32[16,8192]{1,0:T(8,128)S(1)}, f32[16,8192]{1,0:T(8,128)}, u32[]{:S(2)}) copy-start(f32[16,8192]{1,0:T(8,128)} %old_hbm.1) | copy-start | bytes 1572868
  0.7 74.3 %copy-start.2 = (f32[8192]{0:T(1024)S(1)}, f32[8192]{0:T(1024)}, u32[]{:S(2)}) copy-start(f32[8192]{0:T(1024)} %param.12) | copy-start | bytes 98308

commit v4 on v3

--- a/solution.py
+++ b/solution.py
@@ -143,6 +143,24 @@
     for copy in lists:
         copy.start()
     asked[0] = ask_ref[me]
+    pl.semaphore_wait(barrier, others)
+
+    def ask(mask):
+        return remote(ask_ref.at[me ^ mask], asked.at[mask], ask_sent, ask_got, place(mask))
+
+    def give(h, mask):
+        return remote(
+            served.at[h, mask], patches.at[h, mask], sent, got.at[h, mask // width], place(mask)
+        )
+
+    def whole(ref, low, high, sent_sem, got_sem):
+        these = ref.at[pl.ds(low, high - low)]
+        return remote(these, these, sent_sem, got_sem, place(1))
+
+    @functools.partial(partners)
+    def _(mask):
+        ask(mask).start()
+
     loads[0].wait()
 
     @pl.loop(0, tiles, unroll=2)
@@ -151,24 +169,6 @@
             tile = way_ref[8 * h : 8 * h + 8, pl.ds(pl.multiple_of(q * 128, 128), 128)]
             table[0, h, q] = tile
             table[1, h, q] = pltpu.roll(tile, 64, 1)
-
-    pl.semaphore_wait(barrier, others)
-
-    def ask(mask):
-        return remote(ask_ref.at[me ^ mask], asked.at[mask], ask_sent, ask_got, place(mask))
-
-    def give(h, mask):
-        return remote(
-            served.at[h, mask], patches.at[h, mask], sent, got.at[h, mask // width], place(mask)
-        )
-
-    def whole(ref, low, high, sent_sem, got_sem):
-        these = ref.at[pl.ds(low, high - low)]
-        return remote(these, these, sent_sem, got_sem, place(1))
-
-    @functools.partial(partners)
-    def _(mask):
-        ask(mask).start()
 
     whole(asked, 1, devices, ask_sent, ask_got).wait_recv()
     move = pltpu.make_async_copy(asked, numbers, local)
@@ -272,13 +272,10 @@
                 for later in reversed(range(g, PARTS)):
                     offer(1, later)
 
-            @pl.loop(low, high)
+            @pl.loop(low, high, unroll=2)
             def _(mask):
                 scan(h, mask)
 
-        if h == 0:
-            for later in reversed(range(PARTS // 2)):
-                offer(1, later)
 
     forth = [
         remote(tail.at[h], before.at[h], edge_sent.at[h, 0], edge_got.at[h, 0],
@@ -335,7 +332,7 @@
             cells[h, d * per_row + j] = jnp.concatenate([top, values - top], axis=0).astype(jnp.bfloat16)
 
     def filter_all(h):
-        @pl.loop(0, half)
+        @pl.loop(0, half, unroll=2)
         def _(d):
             early, late = before[h, d], after[h, d]
             one_row(h, d, early, pltpu.roll(late, 64, 1))
@@ -372,9 +369,12 @@
     def project_part(h, g):
         low, high = part_of(g)
 
+        @pl.loop(low, high, unroll=min(8, high - low))
+        def _(mask):
+            project(h, mask, part)
+
         @pl.loop(low, high)
         def _(mask):
-            project(h, mask, part)
             send_back(h, mask).start()
 
         if g == 0:
@@ -428,6 +428,8 @@
 
     arrive(0)
     edges(0)
+    for g in reversed(range(PARTS // 2)):
+        offer(1, g)
     edges_in(0)
     filter_all(0)
     for g in reversed(range(PARTS // 2, PARTS)):

time: 77.8 us -> 72.3 us (0.929)
  Pallas kernels: 73.3 us -> 67.7 us
    pallas_call x1, Pallas kernels: 73.3 us -> 67.7 us  [one_step(): pl.pallas_call(functools.partial(step_kernel, groups, spans), out_shape=(...]
where the time goes in v4:
time: 72.3 us; the launch traced here: 71.9 us
  Pallas kernels  67.7 us (94%)
  other arithmetic  2.5 us (3%)
  local copies, waits for them, and re-layouts  0.97 us (1%)
    pallas_call x1, Pallas kernels, one_step(): pl.pallas_call(functools.partial(step_kernel, groups, spans), out_shape=(...  67.7 us
    add x1, other arithmetic, per_device(): new_direction = precond * new_residual + ratio * direction  2.5 us

profile of v4, /device:TPU:0, one launch (start us, length us, event | category | flops | bytes accessed | tf_op | source)
XLA Modules:
  0.0 71.9 jit_solution(6917291972936086425)
XLA Ops:
  0.6 0.0 copy-start
  0.6 0.0 copy-start.1
  0.7 0.0 copy-start.2
  0.7 67.7 %shard_map.112 = (f32[16,8192]{1,0:T(8,128)}, f32[16,128]{1,0:T(8,128)}) custom-call(f32[32]{0:T(128)} %diag_ref.1, s32[8,32]{1,0:T(8,128)} %bitcast.3, f32[16,8192]{1,0:T(8,128)} %way_hbm.1, f32[16,8192]{1,0:T(8,128)} %old_hbm.1, f32[1,8192]{1,0:T(1,128)} %bitcast.2, s32[32,1024]{1,0:T(8,128)} %pixel_hbm.1, f32[32,1024]{1,0:T(8,128)} %gain_hbm.1, ...), custom_call_target="tpu_custom_call" | custom-call | tf_op jit(solution)/shard_map/pallas_call | solution.py:492
  68.4 1.0 %slice_reduce_fusion = (f32[16]{0:T(128)S(1)}, f32[16]{0:T(128)S(1)}) fusion(f32[16,128]{1,0:T(8,128)} %get-tuple-element.5), kind=kLoop, calls=%fused_computation.3 | loop fusion | bytes 256 | tf_op jit(solution)/shard_map/slice | solution.py:562
  69.4 0.0 copy-done
  69.4 0.0 copy-done.1
  69.4 0.0 copy-done.2
  69.4 2.5 %multiply_add_fusion = (f32[16,8192]{1,0:T(8,128)}, f32[16,8192]{1,0:T(8,128)}, f32[16,8192]{1,0:T(8,128)}) fusion(f32[16,8192]{1,0:T(8,128)S(1)} %copy-done, f32[16]{0:T(128)S(1)} %get-tuple-element.7, f32[8192]{0:T(1024)S(1)} %copy-done.2, f32[16,8192]{1,0:T(8,128)S(1)} %copy-done.1, f32[16,8192]{1,0:T(8,128)} %get-tuple-element.6, ...), kind=kLoop, calls=%fused_computation | loop fusion | flops 917504 | bytes 3702912 | tf_op jit(solution)/shard_map/add | solution.py:565
Async XLA Ops:
  0.6 68.7 %copy-start = (f32[16,8192]{1,0:T(8,128)S(1)}, f32[16,8192]{1,0:T(8,128)}, u32[]{:S(2)}) copy-start(f32[16,8192]{1,0:T(8,128)} %way_hbm.1) | copy-start | bytes 1572868
  0.6 68.7 %copy-start.1 = (f32[16,8192]{1,0:T(8,128)S(1)}, f32[16,8192]{1,0:T(8,128)}, u32[]{:S(2)}) copy-start(f32[16,8192]{1,0:T(8,128)} %old_hbm.1) | copy-start | bytes 1572868
  0.7 68.7 %copy-start.2 = (f32[8192]{0:T(1024)S(1)}, f32[8192]{0:T(1024)}, u32[]{:S(2)}) copy-start(f32[8192]{0:T(1024)} %param.12) | copy-start | bytes 98308

commit v5 on v4

--- a/solution.py
+++ b/solution.py
@@ -16,15 +16,11 @@
     return top, (values - top.astype(jnp.float32)).astype(jnp.bfloat16)
 
 
-PARTS = 4
+PARTS = 8
 
 
 def vmem(count):
     return [pl.BlockSpec(memory_space=pltpu.VMEM)] * count
-
-
-def smem(count):
-    return [pl.BlockSpec(memory_space=pltpu.SMEM)] * count
 
 
 def partners_of(groups, spans):
@@ -46,9 +42,9 @@
 
 def step_kernel(
     groups, spans,
-    diag_ref, patch_ref, way_hbm, old_hbm, scale_hbm, pixel_hbm, gain_hbm, band_ref,
+    diag_hbm, patch_hbm, way_hbm, old_hbm, scale_hbm, pixel_hbm, gain_hbm, band_hbm,
     image_ref, factor_ref,
-    way_ref, old_ref, scale_ref, pixel_ref, gain_ref,
+    diag_ref, patch_ref, band_ref, way_ref, old_ref, scale_ref, pixel_ref, gain_ref,
     slot_ref, block_ref, slots, listed, ask_ref, numbers, asked, table, served, patches, pixels, turned, gains, turned_gains, line, bands, hot,
     head, tail, before, after, cells, part, collected, spread, image, sums, held,
     load_sem, ask_sent, ask_got, local, list_sem, sent, got, edge_sent, edge_got, back_sent, back_got,
@@ -71,7 +67,8 @@
     loads = [
         pltpu.make_async_copy(src, dst, load_sem.at[i])
         for i, (src, dst) in enumerate(
-            [(way_hbm, way_ref), (pixel_hbm, pixel_ref), (gain_hbm, gain_ref), (old_hbm, old_ref), (scale_hbm, scale_ref)]
+            [(way_hbm, way_ref), (pixel_hbm, pixel_ref), (gain_hbm, gain_ref), (old_hbm, old_ref), (scale_hbm, scale_ref),
+             (band_hbm, band_ref), (diag_hbm, diag_ref), (patch_hbm, patch_ref)]
         )
     ]
     barrier = pltpu.get_barrier_semaphore()
@@ -85,7 +82,7 @@
     def _(mask):
         pl.semaphore_signal(barrier, inc=1, device_id=place(mask), device_id_type=MESH)
 
-    for load in loads:
+    for load in reversed(loads):
         load.start()
 
     lane8 = lax.broadcasted_iota(jnp.int32, (8, 128), 1)
@@ -104,6 +101,7 @@
     def down(values):
         return jnp.sum(values, axis=0, keepdims=True)
 
+    loads[7].wait()
     padded = jnp.concatenate([patch_ref[...], jnp.zeros((per_row, 128 - rows), jnp.int32)], axis=1)
     repeated = jnp.take_along_axis(padded, lane8 & (rows - 1), axis=1)
     lies = [
@@ -212,6 +210,8 @@
         copy.wait()
 
     lane = lax.broadcasted_iota(jnp.int32, (1, 128), 1)
+    loads[5].wait()
+    loads[6].wait()
     band = jnp.concatenate([band_ref[...], jnp.zeros((rows, 128 - band_ref.shape[1]), jnp.float32)], axis=1)
     wanted = jnp.broadcast_to(jnp.where(lane < 64, 63 - lane, jnp.maximum(lane - 65, 0)), (rows, 128))
     upper = jnp.take_along_axis(band, wanted, axis=1)
@@ -268,9 +268,10 @@
         for g in reversed(range(PARTS)):
             low, high = part_of(g)
             whole(patches.at[h], low, high, sent, got.at[h, g]).wait_recv()
-            if h == 0 and g == PARTS // 2:
-                for later in reversed(range(g, PARTS)):
-                    offer(1, later)
+            if h == 0 and PARTS // 2 <= g < PARTS - 1:
+                offer(1, g + 1)
+                if g == PARTS // 2:
+                    offer(1, g)
 
             @pl.loop(low, high, unroll=2)
             def _(mask):
@@ -478,6 +479,10 @@
         factor_ref[8 * h : 8 * h + 8, :] = jnp.where(lanes == 0, step_size, norm_new / norm_old)
 
 
+def stay(array):
+    return pltpu.with_memory_space_constraint(array, pltpu.HBM)
+
+
 def one_step(diag, patch, way, old, scale, pixels, gains, band, groups, spans):
     devices = groups * spans
     rows = pixels.shape[0]
@@ -495,9 +500,12 @@
             jax.ShapeDtypeStruct(way.shape, jnp.float32),
             jax.ShapeDtypeStruct((way.shape[0], 128), jnp.float32),
         ),
-        in_specs=smem(1) + vmem(1) + [pl.BlockSpec(memory_space=pltpu.HBM)] * 5 + vmem(1),
+        in_specs=[pl.BlockSpec(memory_space=pltpu.HBM)] * 8,
         out_specs=tuple(vmem(2)),
         scratch_shapes=[
+            pltpu.SMEM(diag.shape, jnp.float32),
+            pltpu.VMEM(patch.shape, jnp.int32),
+            pltpu.VMEM(band.shape, jnp.float32),
             pltpu.VMEM(way.shape, jnp.float32),
             pltpu.VMEM(old.shape, jnp.float32),
             pltpu.VMEM(scale.shape, jnp.float32),
@@ -531,7 +539,7 @@
             pltpu.VMEM((2 * tiles * 8, 128), jnp.float32),
             pltpu.VMEM((1, 128), jnp.float32),
             pltpu.VMEM((devices, 1, 128), jnp.float32),
-            dma((5,)),
+            dma((8,)),
             dma,
             dma,
             dma,
@@ -546,7 +554,7 @@
             dma,
         ],
         compiler_params=pltpu.CompilerParams(
-            collective_id=0, has_side_effects=True, vmem_limit_bytes=62 * 1024 * 1024
+            collective_id=0, has_side_effects=True, vmem_limit_bytes=32 * 1024 * 1024
         ),
     )(diag, patch, way, old, scale, pixels, gains, band)
 
@@ -556,8 +564,8 @@
 ):
     groups, spans = lax.axis_size("det"), lax.axis_size("tm")
     image_map, factor = one_step(
-        filter_diag, patch_ids.T, direction, residual, precond[None, :],
-        pixel_in, weights, filter_band, groups, spans,
+        *map(stay, (filter_diag, patch_ids.T, direction, residual, precond[None, :])),
+        *map(stay, (pixel_in, weights, filter_band)), groups, spans,
     )
     step_size, ratio = factor[:, 0:1], factor[:, 1:2]
     new_iterate = iterate + step_size * direction

time: 72.3 us -> 68 us (0.941)
  Pallas kernels: 67.7 us -> 64.6 us
  local copies, waits for them, and re-layouts: 0.97 us -> 0.18 us
    pallas_call x1, Pallas kernels: 67.7 us -> 64.6 us  [one_step(): pl.pallas_call(functools.partial(step_kernel, groups, spans), out_shape=(...]
    slice x1, local copies, waits for them, and re-layouts: 0.95 us -> 0.17 us  [per_device(): step_size, ratio = (factor[:, 0:1], factor[:, 1:2])]
where the time goes in v5:
time: 68 us; the launch traced here: 67.9 us
  Pallas kernels  64.6 us (95%)
  other arithmetic  2.37 us (3%)
  between operations  0.69 us (1%)
    pallas_call x1, Pallas kernels, one_step(): pl.pallas_call(functools.partial(step_kernel, groups, spans), out_shape=(...  64.6 us
    add x1, other arithmetic, per_device(): new_direction = precond * new_residual + ratio * direction  2.37 us

profile of v5, /device:TPU:0, one launch (start us, length us, event | category | flops | bytes accessed | tf_op | source)
XLA Modules:
  0.0 67.9 jit_solution(5074326889887107996)
XLA Ops:
  0.6 0.0 copy-start
  0.6 0.0 copy-start.1
  0.7 0.0 copy-start.2
  0.7 64.6 %shard_map.112 = (f32[16,8192]{1,0:T(8,128)S(1)}, f32[16,128]{1,0:T(8,128)S(1)}) custom-call(f32[32]{0:T(128)} %diag_hbm.1, s32[8,32]{1,0:T(8,128)} %bitcast.3, f32[16,8192]{1,0:T(8,128)} %way_hbm.1, f32[16,8192]{1,0:T(8,128)} %old_hbm.1, f32[1,8192]{1,0:T(1,128)} %bitcast.2, s32[32,1024]{1,0:T(8,128)} %pixel_hbm.1, f32[32,1024]{1,0:T(8,128)} %gain_hbm.1, ...), custom_call_target="tpu_custom_call" | custom-call | tf_op jit(solution)/shard_map/pallas_call | solution.py:497
  65.3 0.2 slice_reduce_fusion
  65.5 0.0 copy-done
  65.5 0.0 copy-done.1
  65.5 0.0 copy-done.2
  65.5 2.4 %multiply_add_fusion = (f32[16,8192]{1,0:T(8,128)}, f32[16,8192]{1,0:T(8,128)}, f32[16,8192]{1,0:T(8,128)}) fusion(f32[16,8192]{1,0:T(8,128)S(1)} %copy-done, f32[16]{0:T(128)S(1)} %get-tuple-element.7, f32[8192]{0:T(1024)S(1)} %copy-done.2, f32[16,8192]{1,0:T(8,128)S(1)} %copy-done.1, f32[16,8192]{1,0:T(8,128)S(1)} %get-tuple-element.6, ...), kind=kLoop, calls=%fused_computation | loop fusion | flops 917504 | bytes 3702912 | tf_op jit(solution)/shard_map/add | solution.py:573
Async XLA Ops:
  0.6 64.8 %copy-start = (f32[16,8192]{1,0:T(8,128)S(1)}, f32[16,8192]{1,0:T(8,128)}, u32[]{:S(2)}) copy-start(f32[16,8192]{1,0:T(8,128)} %way_hbm.1) | copy-start | bytes 1572868
  0.6 64.8 %copy-start.1 = (f32[16,8192]{1,0:T(8,128)S(1)}, f32[16,8192]{1,0:T(8,128)}, u32[]{:S(2)}) copy-start(f32[16,8192]{1,0:T(8,128)} %old_hbm.1) | copy-start | bytes 1572868
  0.7 64.8 %copy-start.2 = (f32[8192]{0:T(1024)S(1)}, f32[8192]{0:T(1024)}, u32[]{:S(2)}) copy-start(f32[8192]{0:T(1024)} %param.12) | copy-start | bytes 98308

commit v6 on v5

--- a/solution.py
+++ b/solution.py
@@ -42,8 +42,8 @@
 
 def step_kernel(
     groups, spans,
-    diag_hbm, patch_hbm, way_hbm, old_hbm, scale_hbm, pixel_hbm, gain_hbm, band_hbm,
-    image_ref, factor_ref,
+    diag_hbm, patch_hbm, at_hbm, way_hbm, old_hbm, scale_hbm, pixel_hbm, gain_hbm, band_hbm,
+    image_ref, factor_ref, at_ref,
     diag_ref, patch_ref, band_ref, way_ref, old_ref, scale_ref, pixel_ref, gain_ref,
     slot_ref, block_ref, slots, listed, ask_ref, numbers, asked, table, served, patches, pixels, turned, gains, turned_gains, line, bands, hot,
     head, tail, before, after, cells, part, collected, spread, image, sums, held,
@@ -68,7 +68,7 @@
         pltpu.make_async_copy(src, dst, load_sem.at[i])
         for i, (src, dst) in enumerate(
             [(way_hbm, way_ref), (pixel_hbm, pixel_ref), (gain_hbm, gain_ref), (old_hbm, old_ref), (scale_hbm, scale_ref),
-             (band_hbm, band_ref), (diag_hbm, diag_ref), (patch_hbm, patch_ref)]
+             (band_hbm, band_ref), (diag_hbm, diag_ref), (patch_hbm, patch_ref), (at_hbm, at_ref)]
         )
     ]
     barrier = pltpu.get_barrier_semaphore()
@@ -82,8 +82,8 @@
     def _(mask):
         pl.semaphore_signal(barrier, inc=1, device_id=place(mask), device_id_type=MESH)
 
-    for load in reversed(loads):
-        load.start()
+    for i in (7, 0, 1, 2, 5, 6, 3, 4, 8):
+        loads[i].start()
 
     lane8 = lax.broadcasted_iota(jnp.int32, (8, 128), 1)
     row8 = lax.broadcasted_iota(jnp.int32, (8, 128), 0)
@@ -448,6 +448,7 @@
         whole(served.at[h], 1, devices, sent, sent).wait_send()
     loads[3].wait()
     loads[4].wait()
+    loads[8].wait()
 
     lanes = lax.broadcasted_iota(jnp.int32, (8, 128), 1)
     places = lax.broadcasted_iota(jnp.int32, (8, 128), 0)
@@ -483,7 +484,7 @@
     return pltpu.with_memory_space_constraint(array, pltpu.HBM)
 
 
-def one_step(diag, patch, way, old, scale, pixels, gains, band, groups, spans):
+def one_step(diag, patch, at, way, old, scale, pixels, gains, band, groups, spans):
     devices = groups * spans
     rows = pixels.shape[0]
     blocks = patch.size
@@ -499,9 +500,10 @@
         out_shape=(
             jax.ShapeDtypeStruct(way.shape, jnp.float32),
             jax.ShapeDtypeStruct((way.shape[0], 128), jnp.float32),
+            jax.ShapeDtypeStruct(at.shape, jnp.float32),
         ),
-        in_specs=[pl.BlockSpec(memory_space=pltpu.HBM)] * 8,
-        out_specs=tuple(vmem(2)),
+        in_specs=[pl.BlockSpec(memory_space=pltpu.HBM)] * 9,
+        out_specs=tuple(vmem(3)),
         scratch_shapes=[
             pltpu.SMEM(diag.shape, jnp.float32),
             pltpu.VMEM(patch.shape, jnp.int32),
@@ -539,7 +541,7 @@
             pltpu.VMEM((2 * tiles * 8, 128), jnp.float32),
             pltpu.VMEM((1, 128), jnp.float32),
             pltpu.VMEM((devices, 1, 128), jnp.float32),
-            dma((8,)),
+            dma((9,)),
             dma,
             dma,
             dma,
@@ -556,19 +558,19 @@
         compiler_params=pltpu.CompilerParams(
             collective_id=0, has_side_effects=True, vmem_limit_bytes=32 * 1024 * 1024
         ),
-    )(diag, patch, way, old, scale, pixels, gains, band)
+    )(diag, patch, at, way, old, scale, pixels, gains, band)
 
 
 def per_device(
     iterate, residual, direction, precond, patch_ids, pixel_in, weights, filter_diag, filter_band
 ):
     groups, spans = lax.axis_size("det"), lax.axis_size("tm")
-    image_map, factor = one_step(
-        *map(stay, (filter_diag, patch_ids.T, direction, residual, precond[None, :])),
+    image_map, factor, kept = one_step(
+        *map(stay, (filter_diag, patch_ids.T, iterate, direction, residual, precond[None, :])),
         *map(stay, (pixel_in, weights, filter_band)), groups, spans,
     )
     step_size, ratio = factor[:, 0:1], factor[:, 1:2]
-    new_iterate = iterate + step_size * direction
+    new_iterate = kept + step_size * direction
     new_residual = residual - step_size * image_map
     new_direction = precond * new_residual + ratio * direction
     return (new_iterate, new_residual, new_direction)

time: 68 us -> 67 us (0.985)
  other arithmetic: 2.37 us -> 1.33 us
    add x1, other arithmetic: 2.37 us -> 1.33 us  [per_device(): new_direction = precond * new_residual + ratio * direction]
where the time goes in v6:
time: 67 us; the launch traced here: 66.8 us
  Pallas kernels  64.6 us (96%)
  other arithmetic  1.33 us (2%)
  between operations  0.69 us (1%)
    pallas_call x1, Pallas kernels, one_step(): pl.pallas_call(functools.partial(step_kernel, groups, spans), out_shape=(...  64.6 us

profile of v6, /device:TPU:0, one launch (start us, length us, event | category | flops | bytes accessed | tf_op | source)
XLA Modules:
  0.0 66.8 jit_solution(4997170951212664787)
XLA Ops:
  0.6 0.0 copy-start
  0.6 0.0 copy-start.1
  0.7 0.0 copy-start.2
  0.7 64.6 %shard_map.112 = (f32[16,8192]{1,0:T(8,128)S(1)}, f32[16,128]{1,0:T(8,128)S(1)}, f32[16,8192]{1,0:T(8,128)S(1)}) custom-call(f32[32]{0:T(128)} %diag_hbm.1, s32[8,32]{1,0:T(8,128)} %bitcast.3, f32[16,8192]{1,0:T(8,128)} %at_hbm.1, f32[16,8192]{1,0:T(8,128)} %way_hbm.1, f32[16,8192]{1,0:T(8,128)} %old_hbm.1, f32[1,8192]{1,0:T(1,128)} %bitcast.2, ...), custom_call_target="tpu_custom_call" | custom-call | tf_op jit(solution)/shard_map/pallas_call | solution.py:498
  65.3 0.2 slice_reduce_fusion
  65.5 0.0 copy-done
  65.5 0.0 copy-done.1
  65.5 0.0 copy-done.2
  65.5 1.3 %multiply_add_fusion = (f32[16,8192]{1,0:T(8,128)}, f32[16,8192]{1,0:T(8,128)}, f32[16,8192]{1,0:T(8,128)}) fusion(f32[16,8192]{1,0:T(8,128)S(1)} %copy-done, f32[16]{0:T(128)S(1)} %get-tuple-element.9, f32[8192]{0:T(1024)S(1)} %copy-done.2, f32[16,8192]{1,0:T(8,128)S(1)} %copy-done.1, f32[16,8192]{1,0:T(8,128)S(1)} %get-tuple-element.8, ...), kind=kLoop, calls=%fused_computation | loop fusion | flops 917504 | bytes 3702912 | tf_op jit(solution)/shard_map/add | solution.py:575
Async XLA Ops:
  0.6 64.8 %copy-start = (f32[16,8192]{1,0:T(8,128)S(1)}, f32[16,8192]{1,0:T(8,128)}, u32[]{:S(2)}) copy-start(f32[16,8192]{1,0:T(8,128)} %way_hbm.1) | copy-start | bytes 1572868
  0.6 64.8 %copy-start.1 = (f32[16,8192]{1,0:T(8,128)S(1)}, f32[16,8192]{1,0:T(8,128)}, u32[]{:S(2)}) copy-start(f32[16,8192]{1,0:T(8,128)} %old_hbm.1) | copy-start | bytes 1572868
  0.7 64.8 %copy-start.2 = (f32[8192]{0:T(1024)S(1)}, f32[8192]{0:T(1024)}, u32[]{:S(2)}) copy-start(f32[8192]{0:T(1024)} %param.12) | copy-start | bytes 98308

commit v7 on v6

--- a/solution.py
+++ b/solution.py
@@ -46,7 +46,7 @@
     image_ref, factor_ref, at_ref,
     diag_ref, patch_ref, band_ref, way_ref, old_ref, scale_ref, pixel_ref, gain_ref,
     slot_ref, block_ref, slots, listed, ask_ref, numbers, asked, table, served, patches, pixels, turned, gains, turned_gains, line, bands, hot,
-    head, tail, before, after, cells, part, collected, spread, image, sums, held,
+    head, tail, before, after, cells, part, collected, spread, image, lean_ref, sums, held,
     load_sem, ask_sent, ask_got, local, list_sem, sent, got, edge_sent, edge_got, back_sent, back_got,
     sum_sent, sum_got,
 ):
@@ -251,7 +251,7 @@
     target = jnp.where(first, 2 * column, 2 * (column - tiles) + 1)
     straight = jnp.where(jnp.where(first, even, odd) == target, 1.0, 0.0)
     crossed = jnp.where(jnp.where(first, odd, even) == target, 1.0, 0.0)
-    spread[...] = jnp.concatenate([straight.T, crossed.T], axis=1).astype(jnp.bfloat16)
+    spread[...] = jnp.concatenate([straight.T, crossed.T] * 2, axis=1).astype(jnp.bfloat16)
 
     def scan(h, mask):
         for i in range(pairs):
@@ -272,6 +272,8 @@
                 offer(1, g + 1)
                 if g == PARTS // 2:
                     offer(1, g)
+                    for later in reversed(range(PARTS // 2)):
+                        offer(1, later)
 
             @pl.loop(low, high, unroll=2)
             def _(mask):
@@ -364,7 +366,7 @@
     def send_back(h, mask):
         these = rows_of(h, mask, 1)
         return remote(
-            part.at[these], collected.at[these], back_sent, back_got.at[h, mask // width], place(mask)
+            part.at[these], collected.at[these], back_sent, back_got.at[h], place(mask)
         )
 
     def project_part(h, g):
@@ -382,13 +384,11 @@
             project(h, 0, collected)
 
     def gather_up(h):
-        for g in reversed(range(PARTS)):
-            low, high = part_of(g)
-            these = collected.at[rows_of(h, low, high - low)]
-            remote(these, these, back_sent, back_got.at[h, g], place(1)).wait_recv()
+        arrived = collected.at[rows_of(h, 1, others)]
+        remote(arrived, arrived, back_sent, back_got.at[h], place(1)).wait_recv()
 
         wide_left = lax.broadcasted_iota(jnp.int32, (tiles, 128), 1) < 64
-        for k in range(8):
+        def column_of(k):
             came = jnp.concatenate(
                 [
                     collected[pl.ds(h * devices * deep + 8 * i + k, devices, stride=deep), :]
@@ -396,14 +396,18 @@
                 ],
                 axis=0,
             )
-            came = jnp.concatenate([came, pltpu.roll(came, 64, 1)], axis=0)
-            total = jnp.dot(
-                spread[...], jnp.concatenate(halves(came), axis=1), preferred_element_type=jnp.float32
+            return jnp.concatenate(halves(jnp.concatenate([came, pltpu.roll(came, 64, 1)], axis=0)), axis=0)
+
+        for k in range(0, 8, 2):
+            both = jnp.dot(
+                spread[...], jnp.concatenate([column_of(k), column_of(k + 1)], axis=1),
+                preferred_element_type=jnp.float32,
             )
-            total = total[:, :128] + total[:, 128:]
-            image[pl.ds(h * tiles * 8 + k, tiles, stride=8), :] = jnp.where(
-                wide_left, total[:tiles], total[tiles:]
-            )
+            for i in range(2):
+                total = both[:, 128 * i : 128 * i + 128]
+                image[pl.ds(h * tiles * 8 + k + i, tiles, stride=8), :] = jnp.where(
+                    wide_left, total[:tiles], total[tiles:]
+                )
 
         zero = jnp.zeros((8, 128), jnp.float32)
 
@@ -411,26 +415,18 @@
             these = pl.ds(pl.multiple_of(q * 128, 128), 128)
             tile = image[pl.ds(pl.multiple_of((h * tiles + q) * 8, 8), 8), :]
             image_ref[8 * h : 8 * h + 8, these] = tile
-            old = old_ref[8 * h : 8 * h + 8, these]
-            scale = jnp.broadcast_to(scale_ref[:, these], (8, 128))
             way = way_ref[8 * h : 8 * h + 8, these]
-            lean = scale * old
-            return (
-                totals[0] + old * lean,
-                totals[1] + way * tile,
-                totals[2] + tile * lean,
-                totals[3] + tile * (scale * tile),
-            )
+            lean = lean_ref[8 * h : 8 * h + 8, these]
+            scaled = jnp.broadcast_to(scale_ref[:, these], (8, 128)) * tile
+            return totals[0] + way * tile, totals[1] + tile * lean, totals[2] + tile * scaled
 
         return [
             jnp.sum(total, axis=1, keepdims=True)
-            for total in lax.fori_loop(0, tiles, add, (zero,) * 4, unroll=4)
+            for total in lax.fori_loop(0, tiles, add, (zero,) * 3, unroll=8)
         ]
 
     arrive(0)
     edges(0)
-    for g in reversed(range(PARTS // 2)):
-        offer(1, g)
     edges_in(0)
     filter_all(0)
     for g in reversed(range(PARTS // 2, PARTS)):
@@ -450,11 +446,27 @@
     loads[4].wait()
     loads[8].wait()
 
+    def lean_on(q, totals):
+        these = pl.ds(pl.multiple_of(q * 128, 128), 128)
+        scale = jnp.broadcast_to(scale_ref[:, these], (8, 128))
+        made = []
+        for h in range(2):
+            old = old_ref[8 * h : 8 * h + 8, these]
+            lean = scale * old
+            lean_ref[8 * h : 8 * h + 8, these] = lean
+            made.append(totals[h] + old * lean)
+        return tuple(made)
+
+    norms = [
+        jnp.sum(total, axis=1, keepdims=True)
+        for total in lax.fori_loop(0, tiles, lean_on, (jnp.zeros((8, 128), jnp.float32),) * 2, unroll=4)
+    ]
+
     lanes = lax.broadcasted_iota(jnp.int32, (8, 128), 1)
     places = lax.broadcasted_iota(jnp.int32, (8, 128), 0)
     row = jnp.zeros((8, 128), jnp.float32)
     for h in range(2):
-        for i, total in enumerate(gather_up(h)):
+        for i, total in enumerate([norms[h]] + gather_up(h)):
             row = jnp.where(lanes == places * 8 + 4 * h + i, total, row)
     sums[...] = jnp.sum(row, axis=0, keepdims=True)
 
@@ -537,8 +549,9 @@
             pltpu.VMEM((2, blocks, 16, 128), jnp.bfloat16),
             pltpu.VMEM(flat, jnp.float32),
             pltpu.VMEM(flat, jnp.float32),
-            pltpu.VMEM((2 * tiles, blocks), jnp.bfloat16),
+            pltpu.VMEM((2 * tiles, 2 * blocks), jnp.bfloat16),
             pltpu.VMEM((2 * tiles * 8, 128), jnp.float32),
+            pltpu.VMEM(way.shape, jnp.float32),
             pltpu.VMEM((1, 128), jnp.float32),
             pltpu.VMEM((devices, 1, 128), jnp.float32),
             dma((9,)),
@@ -551,7 +564,7 @@
             dma((2, 2)),
             dma((2, 2)),
             dma,
-            dma((2, PARTS)),
+            dma((2,)),
             dma,
             dma,
         ],

time: 67 us -> 66.6 us (level)
  no operation moved by 1% of the time
where the time goes in v7:
time: 66.6 us; the launch traced here: 66.5 us
  Pallas kernels  64.3 us (97%)
  other arithmetic  1.33 us (2%)
  between operations  0.69 us (1%)
    pallas_call x1, Pallas kernels, one_step(): pl.pallas_call(functools.partial(step_kernel, groups, spans), out_shape=(...  64.3 us

profile of v7, /device:TPU:0, one launch (start us, length us, event | category | flops | bytes accessed | tf_op | source)
XLA Modules:
  0.0 66.5 jit_solution(18397194655953863776)
XLA Ops:
  0.6 0.0 copy-start
  0.6 0.0 copy-start.1
  0.7 0.0 copy-start.2
  0.7 64.3 %shard_map.112 = (f32[16,8192]{1,0:T(8,128)S(1)}, f32[16,128]{1,0:T(8,128)S(1)}, f32[16,8192]{1,0:T(8,128)S(1)}) custom-call(f32[32]{0:T(128)} %diag_hbm.1, s32[8,32]{1,0:T(8,128)} %bitcast.3, f32[16,8192]{1,0:T(8,128)} %at_hbm.1, f32[16,8192]{1,0:T(8,128)} %way_hbm.1, f32[16,8192]{1,0:T(8,128)} %old_hbm.1, f32[1,8192]{1,0:T(1,128)} %bitcast.2, ...), custom_call_target="tpu_custom_call" | custom-call | tf_op jit(solution)/shard_map/pallas_call | solution.py:510
  65.0 0.2 slice_reduce_fusion
  65.1 0.0 copy-done
  65.1 0.0 copy-done.1
  65.2 0.0 copy-done.2
  65.2 1.3 %multiply_add_fusion = (f32[16,8192]{1,0:T(8,128)}, f32[16,8192]{1,0:T(8,128)}, f32[16,8192]{1,0:T(8,128)}) fusion(f32[16,8192]{1,0:T(8,128)S(1)} %copy-done, f32[16]{0:T(128)S(1)} %get-tuple-element.9, f32[8192]{0:T(1024)S(1)} %copy-done.2, f32[16,8192]{1,0:T(8,128)S(1)} %copy-done.1, f32[16,8192]{1,0:T(8,128)S(1)} %get-tuple-element.8, ...), kind=kLoop, calls=%fused_computation | loop fusion | flops 917504 | bytes 3702912 | tf_op jit(solution)/shard_map/add | solution.py:588
Async XLA Ops:
  0.6 64.5 %copy-start = (f32[16,8192]{1,0:T(8,128)S(1)}, f32[16,8192]{1,0:T(8,128)}, u32[]{:S(2)}) copy-start(f32[16,8192]{1,0:T(8,128)} %way_hbm.1) | copy-start | bytes 1572868
  0.6 64.5 %copy-start.1 = (f32[16,8192]{1,0:T(8,128)S(1)}, f32[16,8192]{1,0:T(8,128)}, u32[]{:S(2)}) copy-start(f32[16,8192]{1,0:T(8,128)} %old_hbm.1) | copy-start | bytes 1572868
  0.7 64.5 %copy-start.2 = (f32[8192]{0:T(1024)S(1)}, f32[8192]{0:T(1024)}, u32[]{:S(2)}) copy-start(f32[8192]{0:T(1024)} %param.12) | copy-start | bytes 98308

commit v8 on v7

--- a/solution.py
+++ b/solution.py
@@ -155,8 +155,7 @@
         these = ref.at[pl.ds(low, high - low)]
         return remote(these, these, sent_sem, got_sem, place(1))
 
-    @functools.partial(partners)
-    def _(mask):
+    for mask in range(others, 0, -1):
         ask(mask).start()
 
     loads[0].wait()
@@ -473,8 +472,7 @@
     def give_sums(mask):
         return remote(sums, held.at[mask], sum_sent, sum_got, place(mask))
 
-    @functools.partial(partners)
-    def _(mask):
+    for mask in range(others, 0, -1):
         give_sums(mask).start()
 
     held[0] = sums[...]

time: 66.6 us -> 66.6 us (level)
  no operation moved by 1% of the time
where the time goes in v8:
time: 66.6 us; the launch traced here: 66.5 us
  Pallas kernels  64.3 us (97%)
  other arithmetic  1.33 us (2%)
  between operations  0.69 us (1%)
    pallas_call x1, Pallas kernels, one_step(): pl.pallas_call(functools.partial(step_kernel, groups, spans), out_shape=(...  64.3 us

profile of v8, /device:TPU:0, one launch (start us, length us, event | category | flops | bytes accessed | tf_op | source)
XLA Modules:
  0.0 66.5 jit_solution(8488231523671773896)
XLA Ops:
  0.6 0.0 copy-start
  0.6 0.0 copy-start.1
  0.7 0.0 copy-start.2
  0.7 64.3 %shard_map.112 = (f32[16,8192]{1,0:T(8,128)S(1)}, f32[16,128]{1,0:T(8,128)S(1)}, f32[16,8192]{1,0:T(8,128)S(1)}) custom-call(f32[32]{0:T(128)} %diag_hbm.1, s32[8,32]{1,0:T(8,128)} %bitcast.3, f32[16,8192]{1,0:T(8,128)} %at_hbm.1, f32[16,8192]{1,0:T(8,128)} %way_hbm.1, f32[16,8192]{1,0:T(8,128)} %old_hbm.1, f32[1,8192]{1,0:T(1,128)} %bitcast.2, ...), custom_call_target="tpu_custom_call" | custom-call | tf_op jit(solution)/shard_map/pallas_call | solution.py:508
  64.9 0.2 slice_reduce_fusion
  65.1 0.0 copy-done
  65.1 0.0 copy-done.1
  65.1 0.0 copy-done.2
  65.1 1.3 %multiply_add_fusion = (f32[16,8192]{1,0:T(8,128)}, f32[16,8192]{1,0:T(8,128)}, f32[16,8192]{1,0:T(8,128)}) fusion(f32[16,8192]{1,0:T(8,128)S(1)} %copy-done, f32[16]{0:T(128)S(1)} %get-tuple-element.9, f32[8192]{0:T(1024)S(1)} %copy-done.2, f32[16,8192]{1,0:T(8,128)S(1)} %copy-done.1, f32[16,8192]{1,0:T(8,128)S(1)} %get-tuple-element.8, ...), kind=kLoop, calls=%fused_computation | loop fusion | flops 917504 | bytes 3702912 | tf_op jit(solution)/shard_map/add | solution.py:586
Async XLA Ops:
  0.6 64.5 %copy-start = (f32[16,8192]{1,0:T(8,128)S(1)}, f32[16,8192]{1,0:T(8,128)}, u32[]{:S(2)}) copy-start(f32[16,8192]{1,0:T(8,128)} %way_hbm.1) | copy-start | bytes 1572868
  0.6 64.5 %copy-start.1 = (f32[16,8192]{1,0:T(8,128)S(1)}, f32[16,8192]{1,0:T(8,128)}, u32[]{:S(2)}) copy-start(f32[16,8192]{1,0:T(8,128)} %old_hbm.1) | copy-start | bytes 1572868
  0.7 64.5 %copy-start.2 = (f32[8192]{0:T(1024)S(1)}, f32[8192]{0:T(1024)}, u32[]{:S(2)}) copy-start(f32[8192]{0:T(1024)} %param.12) | copy-start | bytes 98308
